TPU v7x, 32 devices: a whole 2x2x4 slice. The times are simulated.
32 devices in a mesh: slab: 16 (over z, y, x), col: 2 (over core).
Axes of the slice: x: 2, y: 2, z: 4, core: 2. Of those that a mesh axis runs over, the one named last changes fastest.
Arguments:
- displacement: float32 [3, 64, 128, 256], P(None, 'slab', 'col'), may hold values from -6 to 6
- velocity: float32 [3, 64, 128, 256], P(None, 'slab', 'col'), may hold values from -6 to 6
- damage: float32 [64, 128, 256], P('slab', 'col'), may hold values from 0.5 to 1.5
- broken: int32 [2, 64, 128, 256], P(None, 'slab', 'col'), may hold values from 0 to 255, as said below
- counts: int32 [16, 4], replicated, may hold values from 0 to 64, as said below
- bits: int32 [4], replicated, may hold values from 0 to 3, each once
Outputs:
- relocated: float32 [6, 64, 128, 256], P(None, 'slab', 'col')
Inputs may be any that keep to these rules, and one draw needn't show every extreme that they name: Each bit of a plane of broken marks one forward bond as broken. `counts`: in every aligned group of 16 slabs, the slabs at offsets 0, 1, 2, 4 and 8 of the group offer 64 columns in every round. `bits`: each bit 0..3 is used in exactly one round.
All inputs are finite; a program needn't handle non-finite values.
Results may differ from a plain program's by a relative error of at most 0.00002.
Values sent between devices are 32-bit elements; how exact they have to be, the bound alone decides.
A program may use at most 64 MiB of HBM per device.

v0:
```python
import functools
import math

import jax
import jax.numpy as jnp
from jax import lax
from jax.sharding import PartitionSpec as P


def from_partner(block, axis, bit):
    count = lax.axis_size(axis)
    route = []
    for low in range(count):
        high = low | 1 << bit
        if high != low and high < count:
            route += [(low, high), (high, low)]
    return lax.ppermute(block, axis, route)


def shifted(block, axis, distance):
    devices = range(lax.axis_size(axis))
    route = [(i - distance, i) for i in devices if i - distance in devices]
    return lax.ppermute(block, axis, route)


def padded(block, sides, width):
    for axis, dim in sides:
        count = lax.axis_size(axis)
        forward = [(i, i + 1) for i in range(count - 1)]
        backward = [(target, source) for source, target in forward]
        low = lax.ppermute(
            lax.slice_in_dim(block, block.shape[dim] - width, None, axis=dim), axis, forward
        )
        high = lax.ppermute(lax.slice_in_dim(block, 0, width, axis=dim), axis, backward)
        block = jnp.concatenate([low, block, high], axis=dim)
    return block


def bond_table():
    table = []
    for step_x in range(-2, 3):
        for step_y in range(-2, 3):
            for step_z in range(-2, 3):
                square = step_x * step_x + step_y * step_y + step_z * step_z
                if 0 < square <= 4 and (step_x, step_y, step_z) > (0, 0, 0):
                    length = math.sqrt(square)
                    table.append((step_x, step_y, step_z, (1.0 - length / 2.5) / length**3))
    return table


def bond_term(own_part, other_part, step_x, step_y, step_z, weight, source, bit_index):
    alive = 1.0 - jnp.bitwise_and(jnp.right_shift(source, bit_index), 1).astype(jnp.float32)
    along = (
        step_x * (other_part[0] - own_part[0])
        + step_y * (other_part[1] - own_part[1])
        + step_z * (other_part[2] - own_part[2])
    )
    factor = weight * own_part[3] * other_part[3] * alive * along
    return jnp.stack([factor * step_x, factor * step_y, factor * step_z])


def swap_columns(head, bit_number):
    return from_partner(head, "slab", bit_number)


def on_device(displacement, velocity, damage, broken, counts, bits):
    planes, rows, cells = damage.shape
    fields = jnp.concatenate([displacement, damage[None]], 0)
    forward_data = shifted(fields[:, :2], "slab", -1)
    extended = jnp.concatenate([fields, forward_data], 1)
    extended = padded(extended, (("col", 2),), 2)
    extended = jnp.pad(extended, ((0, 0), (0, 0), (0, 0), (2, 2)))
    own_part = extended[:, 0:planes, 2 : rows + 2, 2 : cells + 2]
    own_force = jnp.zeros((3, planes, rows, cells), jnp.float32)
    reaction = jnp.zeros((3, planes + 2, rows + 4, cells), jnp.float32)
    for index, (step_x, step_y, step_z, weight) in enumerate(bond_table()):
        other_part = extended[
            :,
            step_x : step_x + planes,
            2 + step_y : 2 + step_y + rows,
            2 + step_z : 2 + step_z + cells,
        ]
        term = bond_term(
            own_part, other_part, step_x, step_y, step_z, weight, broken[index // 8], index % 8
        )
        own_force = own_force + term
        placed = lax.pad(
            -term,
            jnp.float32(0.0),
            ((0, 0, 0), (step_x, 2 - step_x, 0), (2 + step_y, 2 - step_y, 0), (step_z, -step_z, 0)),
        )
        reaction = reaction + placed
    position = lax.axis_index("col")
    lower_rim = reaction[:, :, 0:2]
    upper_rim = reaction[:, :, rows + 2 : rows + 4]
    outgoing = jnp.where(position == 0, upper_rim, lower_rim)
    incoming = from_partner(outgoing, "col", 0)
    middle = reaction[:, :, 2 : rows + 2]
    middle = middle.at[:, :, rows - 2 : rows].add(jnp.where(position == 0, incoming, 0.0))
    middle = middle.at[:, :, 0:2].add(jnp.where(position == 1, incoming, 0.0))
    ghost_part = middle[:, planes : planes + 2]
    returned = shifted(ghost_part, "slab", 1)
    force = middle[:, :planes] + own_force
    force = force.at[:, 0:2].add(returned)
    new_velocity = velocity + 0.1 * force
    new_displacement = displacement + 0.1 * new_velocity
    state = jnp.concatenate([new_displacement, new_velocity], 0)
    columns = state.reshape(6, planes * rows, cells)
    capacity = planes * rows // 4
    position = lax.axis_index("slab")
    branches = [
        functools.partial(swap_columns, bit_number=number) for number in range(bits.shape[0])
    ]
    column_index = jnp.arange(capacity, dtype=jnp.int32)
    for round_index in range(bits.shape[0]):
        partner = jnp.bitwise_xor(position, jnp.left_shift(jnp.int32(1), bits[round_index]))
        taken = jnp.minimum(counts[position, round_index], counts[partner, round_index])
        leading = columns[:, :capacity]
        received = lax.switch(bits[round_index], branches, leading)
        leading = jnp.where((column_index < taken)[None, :, None], received, leading)
        columns = columns.at[:, :capacity].set(leading)
    return columns.reshape(6, planes, rows, cells)


def solution(mesh):
    return jax.shard_map(
        on_device,
        mesh=mesh,
        in_specs=(
            P(None, "slab", "col", None),
            P(None, "slab", "col", None),
            P("slab", "col", None),
            P(None, "slab", "col", None),
            P(),
            P(),
        ),
        out_specs=P(None, "slab", "col", None),
        check_vma=False,
    )
```

profile of v0, /device:TPU:0, one launch (start us, length us, event | category | flops | bytes accessed | tf_op | source)
XLA Modules:
  0.0 111.7 jit_solution(13596044810055534008)
XLA Ops:
  0.0 1.2 %pad_maximum_fusion.18 = f32[4,2,64,256]{3,2,1,0:T(8,128)S(1)} fusion(f32[1,4,64,256]{3,2,1,0:T(8,128)} %bitcast.66, f32[3,4,64,256]{3,2,1,0:T(8,128)} %param.36), kind=kLoop, calls=%fused_computation.68 | loop fusion | flops 131072 | bytes 1572864 | tf_op jit(solution)/shard_map/concatenate | solution.py:68
  1.2 1.3 %collective-permute-start.16 = (f32[4,2,64,256]{3,2,1,0:T(8,128)S(1)}, f32[4,2,64,256]{3,2,1,0:T(8,128)S(1)}, u32[]{:S(2)}, u32[]{:S(2)}) collective-permute-start(f32[4,2,64,256]{3,2,1,0:T(8,128)S(1)} %pad_maximum_fusion.18), channel_id=1, source_target_pairs={{2,0},{4,2},{6,4},{8,6},{10,8},{12,10},{14,12},{16,14},{18,16},{20... | collective-permute-start | bytes 1572872 | tf_op jit(solution)/shard_map/ppermute | solution.py:23
  2.5 0.0 copy-done.46
  2.5 0.7 fusion.144
  5.6 0.7 constant_dynamic-slice_fusion.2
  11.2 6.8 %collective-permute-done.16 = f32[4,2,64,256]{3,2,1,0:T(8,128)S(1)} collective-permute-done((f32[4,2,64,256]{3,2,1,0:T(8,128)S(1)}, f32[4,2,64,256]{3,2,1,0:T(8,128)S(1)}, u32[]{:S(2)}, u32[]{:S(2)}) %collective-permute-start.16) | collective-permute-done | bytes 524320 | tf_op jit(solution)/shard_map/ppermute | solution.py:23
  18.0 0.0 copy-done.1
  18.0 1.3 %collective-permute-start.17 = (f32[4,6,2,256]{3,2,1,0:T(2,128)S(1)}, f32[4,6,2,256]{3,2,1,0:T(2,128)S(1)}, u32[]{:S(2)}, u32[]{:S(2)}) collective-permute-start(f32[4,6,2,256]{3,2,1,0:T(2,128)S(1)} %get-tuple-element.177), channel_id=1, source_target_pairs={{0,1},{2,3},{4,5},{6,7},{8,9},{10,11},{12,13},{14,15},{16,17},{18,... | collective-permute-start | bytes 147464 | tf_op jit(solution)/shard_map/ppermute | solution.py:31
  19.3 0.0 copy-start.2
  19.3 1.4 %collective-permute-start.18 = (f32[4,6,2,256]{3,2,1,0:T(2,128)S(1)}, f32[4,6,2,256]{3,2,1,0:T(2,128)S(1)}, u32[]{:S(2)}, u32[]{:S(2)}) collective-permute-start(f32[4,6,2,256]{3,2,1,0:T(2,128)S(1)} %get-tuple-element.178), channel_id=1, source_target_pairs={{1,0},{3,2},{5,4},{7,6},{9,8},{11,10},{13,12},{15,14},{17,16},{19,... | collective-permute-start | bytes 147464 | tf_op jit(solution)/shard_map/ppermute | solution.py:34
  20.8 0.1 pad_maximum_fusion.1
  20.9 0.3 broadcast_multiply_fusion.9
  21.2 0.2 fusion.16
  21.4 0.5 copy-done.4
  21.9 0.7 collective-permute-done.18
  22.6 0.2 pad_maximum_fusion
  22.8 0.4 broadcast_multiply_fusion.15
  23.2 0.0 collective-permute-done.17
  23.2 1.0 select_maximum_fusion
  24.2 0.5 broadcast_multiply_fusion.10
  24.8 1.1 fusion.127
  25.9 0.7 broadcast_multiply_fusion.11
  26.6 0.7 broadcast_multiply_fusion.17
  27.3 0.7 broadcast_multiply_fusion.16
  28.0 0.7 broadcast_multiply_fusion.4
  28.7 0.2 broadcast_multiply_fusion.2
  29.0 1.0 pad_slice_fusion.9
  30.2 0.1 fusion.29
  30.3 0.2 fusion.23
  30.5 0.2 fusion.19
  30.7 0.2 fusion.18
  30.9 0.0 copy-done.42
  31.0 0.2 fusion.26
  31.2 0.2 fusion.21
  31.4 0.2 fusion.17
  31.6 5.5 %fusion.15 = f32[3,6,68,256]{3,2,1,0:T(8,128)S(1)} fusion(f32[3,4,64,256]{3,2,1,0:T(8,128)S(1)} %get-tuple-element.192, f32[3,4,64,256]{3,2,1,0:T(8,128)S(1)} %get-tuple-element.193, f32[3,4,64,256]{3,2,1,0:T(8,128)S(1)} %get-tuple-element.194, f32[3,4,64,256]{3,2,1,0:T(8,128)S(1)} %get-tuple-element.196, f32[3,4,64,256]{3,2,1,0:T(8,128)S(1)} %get-tuple-element.198, ...), kind=kLoop, calls=%fused_computation.33 | loop fusion | flops 4700160 | bytes 13467648 | tf_op jit(solution)/shard_map/add | solution.py:92
  37.0 0.6 collective-permute-start.19
  40.2 0.1 slice.805
  40.3 0.0 collective-permute-done.19
  40.4 4.7 %collective-permute-start.20 = (f32[3,2,64,256]{3,2,1,0:T(8,128)S(1)}, f32[3,2,64,256]{3,2,1,0:T(8,128)S(1)}, u32[]{:S(2)}, u32[]{:S(2)}) collective-permute-start(f32[3,2,64,256]{3,2,1,0:T(8,128)S(1)} %slice.812), channel_id=1, source_target_pairs={{0,2},{2,4},{4,6},{6,8},{8,10},{10,12},{12,14},{14,16},{16,18},{18... | collective-permute-start | bytes 1179656 | tf_op jit(solution)/shard_map/ppermute | solution.py:23
  45.3 3.5 %slice_add_fusion = f32[3,4,64,256]{3,2,1,0:T(8,128)S(1)} fusion(f32[3,6,64,256]{3,2,1,0:T(8,128)S(1)} %fusion.125, f32[1,4,64,256]{3,2,1,0:T(8,128)} %copy-done.32, f32[1,4,64,256]{3,2,1,0:T(8,128)S(1)} %copy-done.5, f32[1,4,64,256]{3,2,1,0:T(8,128)S(1)} %copy-done.13, f32[1,4,64,256]{3,2,1,0:T(8,128)S(1)} %copy-done.15, f32[1,4,64,256]{3,2,1,0:T(8,128)} %copy-done.28, ...), kind=kLoop, calls=%fused_computation.34 | loop fusion | flops 9043968 | bytes 10485760 | tf_op jit(solution)/shard_map/add | solution.py:103
  48.8 0.0 copy-start.44
  48.8 4.9 %collective-permute-done.20 = f32[3,2,64,256]{3,2,1,0:T(8,128)S(1)} collective-permute-done((f32[3,2,64,256]{3,2,1,0:T(8,128)S(1)}, f32[3,2,64,256]{3,2,1,0:T(8,128)S(1)}, u32[]{:S(2)}, u32[]{:S(2)}) %collective-permute-start.20) | collective-permute-done | bytes 393248 | tf_op jit(solution)/shard_map/ppermute | solution.py:23
  53.7 0.1 fusion.31
  53.8 0.2 multiply_add_fusion
  54.0 0.1 pad_maximum_fusion.2
  54.1 11.1 %conditional.4 = (f32[6,64,256]{2,1,0:T(8,128)}) conditional(s32[]{:T(128)} %bitcast.11, f32[6,64,256]{2,1,0:T(8,128)S(1)} %slice.813, f32[6,64,256]{2,1,0:T(8,128)S(1)} %slice.813, f32[6,64,256]{2,1,0:T(8,128)S(1)} %slice.813, f32[6,64,256]{2,1,0:T(8,128)S(1)} %slice.813), branch_computations={%region_0.1_spmd, %region_1.2_spmd, %region_2.3_spmd, %region_3.4_... | conditional | bytes 1572912 | solution.py:119
  54.1 2.5 %collective-permute-start = (f32[6,64,256]{2,1,0:T(8,128)S(1)}, f32[6,64,256]{2,1,0:T(8,128)}, u32[]{:S(2)}, u32[]{:S(2)}) collective-permute-start(f32[6,64,256]{2,1,0:T(8,128)S(1)} %param.14), channel_id=1, source_target_pairs={{0,2},{2,0},{4,6},{6,4},{8,10},{10,8},{12,14},{14,12},{16,18},{18,... | collective-permute-start | bytes 1179656 | tf_op jit(solution)/shard_map/cond/branch_0_fun/ppermute | solution.py:17
  56.7 8.6 %collective-permute-done = f32[6,64,256]{2,1,0:T(8,128)} collective-permute-done((f32[6,64,256]{2,1,0:T(8,128)S(1)}, f32[6,64,256]{2,1,0:T(8,128)}, u32[]{:S(2)}, u32[]{:S(2)}) %collective-permute-start) | collective-permute-done | bytes 393248 | tf_op jit(solution)/shard_map/cond/branch_0_fun/ppermute | solution.py:17
  65.2 1.1 broadcast_select_fusion.2
  66.4 21.1 %conditional.5 = (f32[6,64,256]{2,1,0:T(8,128)}) conditional(s32[]{:T(128)} %bitcast.14, f32[6,64,256]{2,1,0:T(8,128)S(1)} %broadcast_select_fusion.2, f32[6,64,256]{2,1,0:T(8,128)S(1)} %broadcast_select_fusion.2, f32[6,64,256]{2,1,0:T(8,128)S(1)} %broadcast_select_fusion.2, ...), branch_computations={%region_4.5_spmd, %region_5.6_spmd, %region_6.7_spmd, %region_7.8_... | conditional | bytes 1572912 | solution.py:119
  66.4 4.7 %collective-permute-start.7 = (f32[6,64,256]{2,1,0:T(8,128)S(1)}, f32[6,64,256]{2,1,0:T(8,128)}, u32[]{:S(2)}, u32[]{:S(2)}) collective-permute-start(f32[6,64,256]{2,1,0:T(8,128)S(1)} %param.21), channel_id=1, source_target_pairs={{0,16},{16,0},{2,18},{18,2},{4,20},{20,4},{6,22},{22,6},{8,24},{24... | collective-permute-start | bytes 1179656 | tf_op jit(solution)/shard_map/cond/branch_3_fun/ppermute | solution.py:17
  71.1 16.4 %collective-permute-done.7 = f32[6,64,256]{2,1,0:T(8,128)} collective-permute-done((f32[6,64,256]{2,1,0:T(8,128)S(1)}, f32[6,64,256]{2,1,0:T(8,128)}, u32[]{:S(2)}, u32[]{:S(2)}) %collective-permute-start.7) | collective-permute-done | bytes 393248 | tf_op jit(solution)/shard_map/cond/branch_3_fun/ppermute | solution.py:17
  87.5 1.1 %constant_dynamic-update-slice_fusion.1 = (f32[6,256,256]{2,1,0:T(8,128)S(1)}, f32[6,64,256]{2,1,0:T(8,128)S(1)}) fusion(f32[6,256,256]{2,1,0:T(8,128)S(1)} %constant_dynamic-update-slice_fusion.2, f32[6,64,256]{2,1,0:T(8,128)} %get-tuple-element.206, f32[6,64,256]{2,1,0:T(8,128)S(1)} %broadcast_select_fusion.2, pred[64]{0:T(512)(128)(4,1)S(1)} %iota_compare_fusion.4), kind=kLoop, calls=%fused_computation.263 | loop fusion | flops 98304 | bytes 1573376 | tf_op jit(solution)/shard_map/scatter | solution.py:121
  88.6 10.1 %conditional.6 = (f32[6,64,256]{2,1,0:T(8,128)}) conditional(s32[]{:T(128)} %bitcast.17, f32[6,64,256]{2,1,0:T(8,128)S(1)} %get-tuple-element.128, f32[6,64,256]{2,1,0:T(8,128)S(1)} %get-tuple-element.128, f32[6,64,256]{2,1,0:T(8,128)S(1)} %get-tuple-element.128, f32[6,64,256]{2,1,0:T(8,128)S(1)} %get-tuple-element.128), branch_computations={%region_8.9_spmd, %region_9.10_spmd, %region_10.11_spmd, %region_1... | conditional | bytes 1572912 | solution.py:119
  88.7 0.7 collective-permute-start.10
  89.3 9.4 %collective-permute-done.10 = f32[6,64,256]{2,1,0:T(8,128)} collective-permute-done((f32[6,64,256]{2,1,0:T(8,128)S(1)}, f32[6,64,256]{2,1,0:T(8,128)}, u32[]{:S(2)}, u32[]{:S(2)}) %collective-permute-start.10) | collective-permute-done | bytes 393248 | tf_op jit(solution)/shard_map/cond/branch_2_fun/ppermute | solution.py:17
  98.8 1.1 %constant_dynamic-update-slice_fusion = (f32[6,256,256]{2,1,0:T(8,128)S(1)}, f32[6,64,256]{2,1,0:T(8,128)S(1)}) fusion(f32[6,256,256]{2,1,0:T(8,128)S(1)} %get-tuple-element.127, f32[6,64,256]{2,1,0:T(8,128)} %get-tuple-element.207, f32[6,64,256]{2,1,0:T(8,128)S(1)} %get-tuple-element.128, pred[64]{0:T(512)(128)(4,1)S(1)} %iota_compare_fusion.3), kind=kLoop, calls=%fused_computation.262 | loop fusion | flops 98304 | bytes 1573376 | tf_op jit(solution)/shard_map/scatter | solution.py:121
  99.9 9.5 %conditional.7 = (f32[6,64,256]{2,1,0:T(8,128)}) conditional(s32[]{:T(128)} %bitcast.20, f32[6,64,256]{2,1,0:T(8,128)S(1)} %get-tuple-element.126, f32[6,64,256]{2,1,0:T(8,128)S(1)} %get-tuple-element.126, f32[6,64,256]{2,1,0:T(8,128)S(1)} %get-tuple-element.126, f32[6,64,256]{2,1,0:T(8,128)S(1)} %get-tuple-element.126), branch_computations={%region_12.13_spmd, %region_13.14_spmd, %region_14.15_spmd, %regio... | conditional | bytes 1572912 | solution.py:119
  99.9 0.5 collective-permute-start.13
  100.4 9.0 %collective-permute-done.13 = f32[6,64,256]{2,1,0:T(8,128)} collective-permute-done((f32[6,64,256]{2,1,0:T(8,128)S(1)}, f32[6,64,256]{2,1,0:T(8,128)}, u32[]{:S(2)}, u32[]{:S(2)}) %collective-permute-start.13) | collective-permute-done | bytes 393248 | tf_op jit(solution)/shard_map/cond/branch_1_fun/ppermute | solution.py:17
  109.4 1.1 select_dynamic-update-slice_fusion
  110.5 0.0 copy-start.3
  110.5 1.1 %copy-done.3 = f32[6,256,256]{2,1,0:T(8,128)} copy-done((f32[6,256,256]{2,1,0:T(8,128)}, f32[6,256,256]{2,1,0:T(8,128)S(1)}, u32[]{:S(2)}) %copy-start.3) | copy-done | bytes 1572888
  (103 shorter events, 0.5 us)
Async XLA Ops:
  0.0 18.0 %copy-start = (f32[3,4,64,256]{3,2,1,0:T(8,128)S(1)}, f32[3,4,64,256]{3,2,1,0:T(8,128)}, u32[]{:S(2)}) copy-start(f32[3,4,64,256]{3,2,1,0:T(8,128)} %param.36) | copy-start | bytes 2359300
  0.0 18.0 %copy-start.1 = (f32[4,64,256]{2,1,0:T(8,128)S(1)}, f32[4,64,256]{2,1,0:T(8,128)}, u32[]{:S(2)}) copy-start(f32[4,64,256]{2,1,0:T(8,128)} %param.38) | copy-start | bytes 786436
  0.0 2.5 %copy-start.46 = (s32[4]{0:T(128)S(1)}, s32[4]{0:T(128)}, u32[]{:S(2)}) copy-start(s32[4]{0:T(128)} %param.41) | copy-start | bytes 52
  0.0 5.6 %copy-start.45 = (s32[16,4]{0,1:T(4,128)S(1)}, s32[16,4]{0,1:T(4,128)}, u32[]{:S(2)}) copy-start(s32[16,4]{0,1:T(4,128)} %param.40) | copy-start | bytes 772
  1.2 16.8 %collective-permute-start.16 = (f32[4,2,64,256]{3,2,1,0:T(8,128)S(1)}, f32[4,2,64,256]{3,2,1,0:T(8,128)S(1)}, u32[]{:S(2)}, u32[]{:S(2)}) collective-permute-start(f32[4,2,64,256]{3,2,1,0:T(8,128)S(1)} %pad_maximum_fusion.18), channel_id=1, source_target_pairs={{2,0},{4,2},{6,4},{8,6},{10,8},{12,10},{14,12},{16,14},{18,16},{20... | collective-permute-start | bytes 1572872 | tf_op jit(solution)/shard_map/ppermute | solution.py:23
  18.0 5.2 %collective-permute-start.17 = (f32[4,6,2,256]{3,2,1,0:T(2,128)S(1)}, f32[4,6,2,256]{3,2,1,0:T(2,128)S(1)}, u32[]{:S(2)}, u32[]{:S(2)}) collective-permute-start(f32[4,6,2,256]{3,2,1,0:T(2,128)S(1)} %get-tuple-element.177), channel_id=1, source_target_pairs={{0,1},{2,3},{4,5},{6,7},{8,9},{10,11},{12,13},{14,15},{16,17},{18,... | collective-permute-start | bytes 147464 | tf_op jit(solution)/shard_map/ppermute | solution.py:31
  19.3 1.6 %copy-start.2 = (s32[2,4,64,256]{3,2,1,0:T(8,128)S(1)}, s32[2,4,64,256]{3,2,1,0:T(8,128)}, u32[]{:S(2)}) copy-start(s32[2,4,64,256]{3,2,1,0:T(8,128)} %param.39) | copy-start | bytes 1572868
  19.3 3.3 %collective-permute-start.18 = (f32[4,6,2,256]{3,2,1,0:T(2,128)S(1)}, f32[4,6,2,256]{3,2,1,0:T(2,128)S(1)}, u32[]{:S(2)}, u32[]{:S(2)}) collective-permute-start(f32[4,6,2,256]{3,2,1,0:T(2,128)S(1)} %get-tuple-element.178), channel_id=1, source_target_pairs={{1,0},{3,2},{5,4},{7,6},{9,8},{11,10},{13,12},{15,14},{17,16},{19,... | collective-permute-start | bytes 147464 | tf_op jit(solution)/shard_map/ppermute | solution.py:34
  21.2 0.7 copy-start.4
  21.2 1.4 %copy-start.32 = (f32[1,4,64,256]{3,2,1,0:T(8,128)}, f32[1,4,64,256]{3,2,1,0:T(8,128)S(1)}, u32[]{:S(2)}) copy-start(f32[1,4,64,256]{3,2,1,0:T(8,128)S(1)} %broadcast_multiply_fusion.20) | copy-start | bytes 786436
  23.2 7.1 %copy-start.6 = (f32[1,4,64,256]{3,2,1,0:T(8,128)}, f32[1,4,64,256]{3,2,1,0:T(8,128)S(1)}, u32[]{:S(2)}) copy-start(f32[1,4,64,256]{3,2,1,0:T(8,128)S(1)} %get-tuple-element.133) | copy-start | bytes 786436
  23.2 7.1 %copy-start.8 = (f32[1,4,64,256]{3,2,1,0:T(8,128)}, f32[1,4,64,256]{3,2,1,0:T(8,128)S(1)}, u32[]{:S(2)}) copy-start(f32[1,4,64,256]{3,2,1,0:T(8,128)S(1)} %get-tuple-element.134) | copy-start | bytes 786436
  23.2 7.1 %copy-start.10 = (f32[1,4,64,256]{3,2,1,0:T(8,128)}, f32[1,4,64,256]{3,2,1,0:T(8,128)S(1)}, u32[]{:S(2)}) copy-start(f32[1,4,64,256]{3,2,1,0:T(8,128)S(1)} %get-tuple-element.171) | copy-start | bytes 786436
  24.7 6.6 %copy-start.12 = (f32[1,4,64,256]{3,2,1,0:T(8,128)}, f32[1,4,64,256]{3,2,1,0:T(8,128)S(1)}, u32[]{:S(2)}) copy-start(f32[1,4,64,256]{3,2,1,0:T(8,128)S(1)} %get-tuple-element.141) | copy-start | bytes 786436
  24.8 6.6 %copy-start.14 = (f32[1,4,64,256]{3,2,1,0:T(8,128)}, f32[1,4,64,256]{3,2,1,0:T(8,128)S(1)}, u32[]{:S(2)}) copy-start(f32[1,4,64,256]{3,2,1,0:T(8,128)S(1)} %get-tuple-element.142) | copy-start | bytes 786436
  24.8 6.6 %copy-start.16 = (f32[1,4,64,256]{3,2,1,0:T(8,128)}, f32[1,4,64,256]{3,2,1,0:T(8,128)S(1)}, u32[]{:S(2)}) copy-start(f32[1,4,64,256]{3,2,1,0:T(8,128)S(1)} %get-tuple-element.175) | copy-start | bytes 786436
  24.8 6.6 %copy-start.18 = (f32[1,4,64,256]{3,2,1,0:T(8,128)}, f32[1,4,64,256]{3,2,1,0:T(8,128)S(1)}, u32[]{:S(2)}) copy-start(f32[1,4,64,256]{3,2,1,0:T(8,128)S(1)} %get-tuple-element.176) | copy-start | bytes 786436
  26.6 4.6 %copy-start.35 = (f32[1,4,64,256]{3,2,1,0:T(8,128)}, f32[1,4,64,256]{3,2,1,0:T(8,128)S(1)}, u32[]{:S(2)}) copy-start(f32[1,4,64,256]{3,2,1,0:T(8,128)S(1)} %get-tuple-element.149) | copy-start | bytes 786436
  26.6 4.6 %copy-start.36 = (f32[1,4,64,256]{3,2,1,0:T(8,128)}, f32[1,4,64,256]{3,2,1,0:T(8,128)S(1)}, u32[]{:S(2)}) copy-start(f32[1,4,64,256]{3,2,1,0:T(8,128)S(1)} %get-tuple-element.167) | copy-start | bytes 786436
  26.6 4.6 %copy-start.37 = (f32[1,4,64,256]{3,2,1,0:T(8,128)}, f32[1,4,64,256]{3,2,1,0:T(8,128)S(1)}, u32[]{:S(2)}) copy-start(f32[1,4,64,256]{3,2,1,0:T(8,128)S(1)} %get-tuple-element.168) | copy-start | bytes 786436
  27.3 3.6 %copy-start.38 = (f32[1,4,64,256]{3,2,1,0:T(8,128)}, f32[1,4,64,256]{3,2,1,0:T(8,128)S(1)}, u32[]{:S(2)}) copy-start(f32[1,4,64,256]{3,2,1,0:T(8,128)S(1)} %get-tuple-element.157) | copy-start | bytes 786436
  27.3 3.6 %copy-start.39 = (f32[1,4,64,256]{3,2,1,0:T(8,128)}, f32[1,4,64,256]{3,2,1,0:T(8,128)S(1)}, u32[]{:S(2)}) copy-start(f32[1,4,64,256]{3,2,1,0:T(8,128)S(1)} %get-tuple-element.169) | copy-start | bytes 786436
  28.0 2.5 %copy-start.20 = (f32[1,4,64,256]{3,2,1,0:T(8,128)}, f32[1,4,64,256]{3,2,1,0:T(8,128)S(1)}, u32[]{:S(2)}) copy-start(f32[1,4,64,256]{3,2,1,0:T(8,128)S(1)} %get-tuple-element.147) | copy-start | bytes 786436
  28.0 2.5 %copy-start.22 = (f32[1,4,64,256]{3,2,1,0:T(8,128)}, f32[1,4,64,256]{3,2,1,0:T(8,128)S(1)}, u32[]{:S(2)}) copy-start(f32[1,4,64,256]{3,2,1,0:T(8,128)S(1)} %get-tuple-element.148) | copy-start | bytes 786436
  28.0 2.5 %copy-start.24 = (f32[1,4,64,256]{3,2,1,0:T(8,128)}, f32[1,4,64,256]{3,2,1,0:T(8,128)S(1)}, u32[]{:S(2)}) copy-start(f32[1,4,64,256]{3,2,1,0:T(8,128)S(1)} %get-tuple-element.165) | copy-start | bytes 786436
  28.0 2.5 %copy-start.26 = (f32[1,4,64,256]{3,2,1,0:T(8,128)}, f32[1,4,64,256]{3,2,1,0:T(8,128)S(1)}, u32[]{:S(2)}) copy-start(f32[1,4,64,256]{3,2,1,0:T(8,128)S(1)} %get-tuple-element.166) | copy-start | bytes 786436
  28.7 2.0 %copy-start.28 = (f32[1,4,64,256]{3,2,1,0:T(8,128)}, f32[1,4,64,256]{3,2,1,0:T(8,128)S(1)}, u32[]{:S(2)}) copy-start(f32[1,4,64,256]{3,2,1,0:T(8,128)S(1)} %get-tuple-element.145) | copy-start | bytes 786436
  28.7 2.0 %copy-start.29 = (f32[1,4,64,256]{3,2,1,0:T(8,128)}, f32[1,4,64,256]{3,2,1,0:T(8,128)S(1)}, u32[]{:S(2)}) copy-start(f32[1,4,64,256]{3,2,1,0:T(8,128)S(1)} %get-tuple-element.146) | copy-start | bytes 786436
  28.7 2.0 %copy-start.30 = (f32[1,4,64,256]{3,2,1,0:T(8,128)}, f32[1,4,64,256]{3,2,1,0:T(8,128)S(1)}, u32[]{:S(2)}) copy-start(f32[1,4,64,256]{3,2,1,0:T(8,128)S(1)} %get-tuple-element.163) | copy-start | bytes 786436
  28.7 2.0 %copy-start.31 = (f32[1,4,64,256]{3,2,1,0:T(8,128)}, f32[1,4,64,256]{3,2,1,0:T(8,128)S(1)}, u32[]{:S(2)}) copy-start(f32[1,4,64,256]{3,2,1,0:T(8,128)S(1)} %get-tuple-element.164) | copy-start | bytes 786436
  29.0 1.2 %copy-start.43 = (f32[1,4,64,256]{3,2,1,0:T(8,128)}, f32[1,4,64,256]{3,2,1,0:T(8,128)S(1)}, u32[]{:S(2)}) copy-start(f32[1,4,64,256]{3,2,1,0:T(8,128)S(1)} %get-tuple-element.137) | copy-start | bytes 786436
  29.0 1.2 %copy-start.34 = (f32[1,4,64,256]{3,2,1,0:T(8,128)}, f32[1,4,64,256]{3,2,1,0:T(8,128)S(1)}, u32[]{:S(2)}) copy-start(f32[1,4,64,256]{3,2,1,0:T(8,128)S(1)} %broadcast_multiply_fusion.12) | copy-start | bytes 786436
  29.0 1.2 %copy-start.33 = (f32[1,4,64,256]{3,2,1,0:T(8,128)}, f32[1,4,64,256]{3,2,1,0:T(8,128)S(1)}, u32[]{:S(2)}) copy-start(f32[1,4,64,256]{3,2,1,0:T(8,128)S(1)} %broadcast_multiply_fusion.13) | copy-start | bytes 786436
  30.1 1.1 copy-start.40
  30.1 0.8 copy-start.41
  30.1 0.8 copy-start.42
  37.0 3.3 %collective-permute-start.19 = (f32[3,6,2,256]{3,2,1,0:T(2,128)S(1)}, f32[3,6,2,256]{3,2,1,0:T(2,128)S(1)}, u32[]{:S(2)}, u32[]{:S(2)}) collective-permute-start(f32[3,6,2,256]{3,2,1,0:T(2,128)S(1)} %slice_select_fusion), channel_id=1, source_target_pairs={{0,1},{1,0},{2,3},{3,2},{4,5},{5,4},{6,7},{7,6},{8,9},{9,8},{10,11... | collective-permute-start | bytes 110600 | tf_op jit(solution)/shard_map/ppermute | solution.py:17
  40.1 5.1 %copy-start.5 = (f32[1,4,64,256]{3,2,1,0:T(8,128)S(1)}, f32[1,4,64,256]{3,2,1,0:T(8,128)}, u32[]{:S(2)}) copy-start(f32[1,4,64,256]{3,2,1,0:T(8,128)} %copy-done.4) | copy-start | bytes 786436
  40.1 5.1 %copy-start.7 = (f32[1,4,64,256]{3,2,1,0:T(8,128)S(1)}, f32[1,4,64,256]{3,2,1,0:T(8,128)}, u32[]{:S(2)}) copy-start(f32[1,4,64,256]{3,2,1,0:T(8,128)} %copy-done.6) | copy-start | bytes 786436
  40.1 5.1 %copy-start.9 = (f32[1,4,64,256]{3,2,1,0:T(8,128)S(1)}, f32[1,4,64,256]{3,2,1,0:T(8,128)}, u32[]{:S(2)}) copy-start(f32[1,4,64,256]{3,2,1,0:T(8,128)} %copy-done.8) | copy-start | bytes 786436
  40.1 5.1 %copy-start.11 = (f32[1,4,64,256]{3,2,1,0:T(8,128)S(1)}, f32[1,4,64,256]{3,2,1,0:T(8,128)}, u32[]{:S(2)}) copy-start(f32[1,4,64,256]{3,2,1,0:T(8,128)} %copy-done.10) | copy-start | bytes 786436
  40.1 5.1 %copy-start.13 = (f32[1,4,64,256]{3,2,1,0:T(8,128)S(1)}, f32[1,4,64,256]{3,2,1,0:T(8,128)}, u32[]{:S(2)}) copy-start(f32[1,4,64,256]{3,2,1,0:T(8,128)} %copy-done.12) | copy-start | bytes 786436
  40.1 5.1 %copy-start.15 = (f32[1,4,64,256]{3,2,1,0:T(8,128)S(1)}, f32[1,4,64,256]{3,2,1,0:T(8,128)}, u32[]{:S(2)}) copy-start(f32[1,4,64,256]{3,2,1,0:T(8,128)} %copy-done.14) | copy-start | bytes 786436
  40.1 5.1 %copy-start.17 = (f32[1,4,64,256]{3,2,1,0:T(8,128)S(1)}, f32[1,4,64,256]{3,2,1,0:T(8,128)}, u32[]{:S(2)}) copy-start(f32[1,4,64,256]{3,2,1,0:T(8,128)} %copy-done.16) | copy-start | bytes 786436
  40.1 5.1 %copy-start.19 = (f32[1,4,64,256]{3,2,1,0:T(8,128)S(1)}, f32[1,4,64,256]{3,2,1,0:T(8,128)}, u32[]{:S(2)}) copy-start(f32[1,4,64,256]{3,2,1,0:T(8,128)} %copy-done.18) | copy-start | bytes 786436
  40.1 5.1 %copy-start.21 = (f32[1,4,64,256]{3,2,1,0:T(8,128)S(1)}, f32[1,4,64,256]{3,2,1,0:T(8,128)}, u32[]{:S(2)}) copy-start(f32[1,4,64,256]{3,2,1,0:T(8,128)} %copy-done.20) | copy-start | bytes 786436
  40.2 5.1 %copy-start.23 = (f32[1,4,64,256]{3,2,1,0:T(8,128)S(1)}, f32[1,4,64,256]{3,2,1,0:T(8,128)}, u32[]{:S(2)}) copy-start(f32[1,4,64,256]{3,2,1,0:T(8,128)} %copy-done.22) | copy-start | bytes 786436
  40.2 5.1 %copy-start.25 = (f32[1,4,64,256]{3,2,1,0:T(8,128)S(1)}, f32[1,4,64,256]{3,2,1,0:T(8,128)}, u32[]{:S(2)}) copy-start(f32[1,4,64,256]{3,2,1,0:T(8,128)} %copy-done.24) | copy-start | bytes 786436
  40.2 5.1 %copy-start.27 = (f32[1,4,64,256]{3,2,1,0:T(8,128)S(1)}, f32[1,4,64,256]{3,2,1,0:T(8,128)}, u32[]{:S(2)}) copy-start(f32[1,4,64,256]{3,2,1,0:T(8,128)} %copy-done.26) | copy-start | bytes 786436
  40.4 13.2 %collective-permute-start.20 = (f32[3,2,64,256]{3,2,1,0:T(8,128)S(1)}, f32[3,2,64,256]{3,2,1,0:T(8,128)S(1)}, u32[]{:S(2)}, u32[]{:S(2)}) collective-permute-start(f32[3,2,64,256]{3,2,1,0:T(8,128)S(1)} %slice.812), channel_id=1, source_target_pairs={{0,2},{2,4},{4,6},{6,8},{8,10},{10,12},{12,14},{14,16},{16,18},{18... | collective-permute-start | bytes 1179656 | tf_op jit(solution)/shard_map/ppermute | solution.py:23
  48.8 5.0 %copy-start.44 = (f32[3,4,64,256]{3,2,1,0:T(8,128)S(1)}, f32[3,4,64,256]{3,2,1,0:T(8,128)}, u32[]{:S(2)}) copy-start(f32[3,4,64,256]{3,2,1,0:T(8,128)} %param.37) | copy-start | bytes 2359300
  54.1 11.1 %collective-permute-start = (f32[6,64,256]{2,1,0:T(8,128)S(1)}, f32[6,64,256]{2,1,0:T(8,128)}, u32[]{:S(2)}, u32[]{:S(2)}) collective-permute-start(f32[6,64,256]{2,1,0:T(8,128)S(1)} %param.14), channel_id=1, source_target_pairs={{0,2},{2,0},{4,6},{6,4},{8,10},{10,8},{12,14},{14,12},{16,18},{18,... | collective-permute-start | bytes 1179656 | tf_op jit(solution)/shard_map/cond/branch_0_fun/ppermute | solution.py:17
  66.4 21.1 %collective-permute-start.7 = (f32[6,64,256]{2,1,0:T(8,128)S(1)}, f32[6,64,256]{2,1,0:T(8,128)}, u32[]{:S(2)}, u32[]{:S(2)}) collective-permute-start(f32[6,64,256]{2,1,0:T(8,128)S(1)} %param.21), channel_id=1, source_target_pairs={{0,16},{16,0},{2,18},{18,2},{4,20},{20,4},{6,22},{22,6},{8,24},{24... | collective-permute-start | bytes 1179656 | tf_op jit(solution)/shard_map/cond/branch_3_fun/ppermute | solution.py:17
  88.7 10.1 %collective-permute-start.10 = (f32[6,64,256]{2,1,0:T(8,128)S(1)}, f32[6,64,256]{2,1,0:T(8,128)}, u32[]{:S(2)}, u32[]{:S(2)}) collective-permute-start(f32[6,64,256]{2,1,0:T(8,128)S(1)} %param.24), channel_id=1, source_target_pairs={{0,8},{8,0},{2,10},{10,2},{4,12},{12,4},{6,14},{14,6},{16,24},{24,... | collective-permute-start | bytes 1179656 | tf_op jit(solution)/shard_map/cond/branch_2_fun/ppermute | solution.py:17
  99.9 9.5 %collective-permute-start.13 = (f32[6,64,256]{2,1,0:T(8,128)S(1)}, f32[6,64,256]{2,1,0:T(8,128)}, u32[]{:S(2)}, u32[]{:S(2)}) collective-permute-start(f32[6,64,256]{2,1,0:T(8,128)S(1)} %param.27), channel_id=1, source_target_pairs={{0,4},{4,0},{2,6},{6,2},{8,12},{12,8},{10,14},{14,10},{16,20},{20,... | collective-permute-start | bytes 1179656 | tf_op jit(solution)/shard_map/cond/branch_1_fun/ppermute | solution.py:17
  110.5 1.1 %copy-start.3 = (f32[6,256,256]{2,1,0:T(8,128)}, f32[6,256,256]{2,1,0:T(8,128)S(1)}, u32[]{:S(2)}) copy-start(f32[6,256,256]{2,1,0:T(8,128)S(1)} %select_dynamic-update-slice_fusion) | copy-start | bytes 4718596
where the time goes:
time: 111 us; the launch traced here: 112 us
  waiting for transfers between devices  55.7 us (50%)
  other arithmetic  23 us (21%)
  starting transfers between devices  17.7 us (16%)
  between operations  10.7 us (10%)
  local copies, waits for them, and re-layouts  4.4 us (4%)
    ppermute x5, waiting for transfers between devices, from_partner(): return lax.ppermute(block, axis, route)  43.4 us
    ppermute x2, waiting for transfers between devices, shifted(): return lax.ppermute(block, axis, route)  11.7 us
    ppermute x5, starting transfers between devices, from_partner(): return lax.ppermute(block, axis, route)  9 us
    ppermute x2, starting transfers between devices, shifted(): return lax.ppermute(block, axis, route)  5.98 us
    add x1, other arithmetic, on_device(): reaction = reaction + placed  5.45 us
    mul x14, other arithmetic, bond_term(): return jnp.stack([factor * step_x, factor * step_y, factor * step_z])  4.31 us
    add x1, other arithmetic, on_device(): force = middle[:, :planes] + own_force  3.5 us
    scatter x3, other arithmetic, on_device(): columns = columns.at[:, :capacity].set(leading)  3.35 us
  transfers between devices with their start and end apart: 9, of which 7 were waited for; matrix products, arithmetic and copies ran while one was open for 6% of the time, Pallas kernels for 0%

commit v1 on v0

v1 whole, which is shorter than its diff:
```python
import functools
import math

import jax
import jax.numpy as jnp
from jax import lax
from jax.experimental import pallas as pl
from jax.experimental.pallas import tpu as pltpu
from jax.sharding import PartitionSpec as P

MESH = pl.DeviceIdType.MESH
PLACE = (0, 2, 3)
BAND = 16
ROUNDS = 4


def bond_table():
    table = []
    for step_x in range(-2, 3):
        for step_y in range(-2, 3):
            for step_z in range(-2, 3):
                square = step_x * step_x + step_y * step_y + step_z * step_z
                if 0 < square <= 4 and (step_x, step_y, step_z) > (0, 0, 0):
                    length = math.sqrt(square)
                    table.append((step_x, step_y, step_z, (1.0 - length / 2.5) / length**3))
    return table


def moved_along_cells(value, step):
    cells = value.shape[-1]
    lane = lax.broadcasted_iota(jnp.int32, value.shape, value.ndim - 1)
    turned = pltpu.roll(value, (-step) % cells, value.ndim - 1)
    inside = (lane < cells - step) if step > 0 else (lane >= -step)
    return jnp.where(inside, turned, jnp.zeros_like(turned))


def kernel(
    taken, bits, rounds_of, displacement, velocity, damage, broken, result,
    fields, flags, fields_low, fields_high, flags_low, flags_high,
    rows_low, rows_high, row_flags_low, row_flags_high, far_low, far_high, far_flags,
    partial, back, returned, stage, arrived, ready_velocity,
    in00, in01, in10, in11, out00, out01, out10, out11,
    col_send, col_recv, down_send, down_recv, back_send, back_recv,
    ride_send, ride_recv,
):
    planes, rows, cells = damage.shape
    half = cells // 2
    slabs = lax.axis_size("slab")
    slab = lax.axis_index("slab")
    col = lax.axis_index("col")
    other = 1 - col
    has_low = slab > 0
    has_high = slab < slabs - 1
    table = bond_table()
    incoming = ((in00, in01), (in10, in11))
    outgoing = ((out00, out01), (out10, out11))

    for component in range(3):
        fields[PLACE[component], 0:planes, 8 : 8 + rows] = displacement[component]
    fields[1, 0:planes, 8 : 8 + rows] = damage[...]
    flags[:, :, 8 : 8 + rows] = broken[...]
    fields[:, 0:planes, 0:8] = jnp.zeros((4, planes, 8, cells), jnp.float32)
    fields[:, 0:planes, 8 + rows : 16 + rows] = jnp.zeros((4, planes, 8, cells), jnp.float32)
    fields[:, planes : planes + 2] = jnp.zeros((4, 2, rows + 16, cells), jnp.float32)
    flags[:, :, 0:8] = jnp.zeros((2, planes, 8, cells), jnp.int32)
    flags[:, :, 8 + rows : 16 + rows] = jnp.zeros((2, planes, 8, cells), jnp.int32)
    returned[...] = jnp.zeros_like(returned)
    stage[...] = jnp.zeros_like(stage)

    partners = []
    for bit in range(ROUNDS):
        weight = 1 << bit
        partners.append(slab + weight - 2 * weight * ((slab // weight) % 2))

    barrier = pltpu.get_barrier_semaphore()

    def greet(to_slab, to_col):
        pl.semaphore_signal(barrier, inc=1, device_id=(to_slab, to_col), device_id_type=MESH)

    greet(slab, other)
    for partner in partners:
        greet(partner, col)

    @pl.when(has_low)
    def _():
        greet(slab - 1, col)
        greet(slab - 1, other)

    @pl.when(has_high)
    def _():
        greet(slab + 1, col)
        greet(slab + 1, other)

    sides = has_low.astype(jnp.int32) + has_high.astype(jnp.int32)
    pl.semaphore_wait(barrier, 1 + ROUNDS + 2 * sides)

    rim = pl.ds(pl.multiple_of(8 + (1 - col) * (rows - 8), 8), 8)
    ghost = pl.ds(pl.multiple_of((8 + rows) * col, 8), 8)

    def remote(source, target, sends, receives, to_slab, to_col):
        return pltpu.make_async_remote_copy(
            src_ref=source, dst_ref=target, send_sem=sends, recv_sem=receives,
            device_id=(to_slab, to_col), device_id_type=MESH,
        )

    beside = [
        remote(fields.at[:, 0:planes, rim], fields.at[:, 0:planes, ghost],
               col_send.at[0], col_recv.at[0], slab, other),
        remote(flags.at[:, :, rim], flags.at[:, :, ghost],
               col_send.at[1], col_recv.at[1], slab, other),
    ]
    inner = pl.ds(8, rows)
    below = [
        remote(fields.at[:, 0, inner], fields.at[:, planes, inner],
               down_send.at[0], down_recv.at[0], slab - 1, col),
        remote(fields.at[:, 0, rim], fields.at[:, planes, ghost],
               down_send.at[1], down_recv.at[1], slab - 1, other),
        remote(fields.at[0:2, 1, inner], fields.at[0:2, planes + 1, inner],
               down_send.at[2], down_recv.at[2], slab - 1, col),
    ]
    above = [
        remote(back.at[0:3], returned.at[0:3], back_send.at[0], back_recv.at[0], slab + 1, col),
        remote(back.at[3], returned.at[3], back_send.at[1], back_recv.at[1], slab + 1, col),
    ]

    @pl.when(has_low)
    def _():
        for copy in below:
            copy.start()

    for copy in beside:
        copy.start()

    column = lax.broadcasted_iota(jnp.int32, (rows, half), 0)

    def rides(pipe, step):
        parity = step % 2
        return [
            remote(outgoing[pipe][parity].at[bit], incoming[pipe][parity].at[bit],
                   ride_send.at[pipe, parity, bit], ride_recv.at[pipe, parity, bit],
                   partners[bit], col)
            for bit in range(ROUNDS)
        ]

    last = 6 + ROUNDS - 1

    def ride(pipe, step):
        lanes = slice(pipe * half, (pipe + 1) * half)
        if step > 0:
            for copy in rides(pipe, step - 1):
                copy.wait_recv()
            source = incoming[pipe][(step - 1) % 2]
            for number in reversed(range(ROUNDS)):
                new = jnp.where(
                    column < taken[number], source[bits[number]], stage[pipe, number]
                )
                if number < ROUNDS - 1:
                    stage[pipe, number + 1] = new
                elif step >= ROUNDS:
                    item = step - ROUNDS
                    if item < 3:
                        arrived[item, :, lanes] = new
                    else:
                        result[item, 0, :, lanes] = new
                        result[item - 3, 0, :, lanes] = arrived[item - 3, :, lanes] + 0.1 * new
        if step < last:
            if step < 3:
                stage[pipe, 0] = displacement[step, 0, :, lanes]
            elif step < 6:
                stage[pipe, 0] = ready_velocity[step - 3, :, lanes]
            if step >= 2:
                for copy in rides(pipe, step - 2):
                    copy.wait_send()
            target = outgoing[pipe][step % 2]
            for bit in range(ROUNDS):
                target[bit] = stage[pipe, rounds_of[bit]]
            for copy in rides(pipe, step):
                copy.start()
        else:
            for back_step in (last - 2, last - 1):
                for copy in rides(pipe, back_step):
                    copy.wait_send()

    def ride_both(step):
        for pipe in range(2):
            ride(pipe, step)

    def shift_plane(plane, with_flags):
        def body(index, carry):
            here = pl.ds(pl.multiple_of(index * 8, 8), 8)
            for field in range(4):
                value = fields[field, plane, here]
                fields_low[field, plane, here] = moved_along_cells(value, -1)
                fields_high[field, plane, here] = moved_along_cells(value, 1)
            if with_flags:
                for part in range(2):
                    value = flags[part, plane, here]
                    flags_low[part, plane, here] = moved_along_cells(value, -1)
                    flags_high[part, plane, here] = moved_along_cells(value, 1)
            return carry

        lax.fori_loop(0, (rows + 16) // 8, body, 0)

        def field_rows(field, carry):
            for place, source in enumerate((fields_low, fields, fields_high)):
                rows_low[place, field, plane] = source[field, plane, 7 : 7 + rows]
                rows_high[place, field, plane] = source[field, plane, 9 : 9 + rows]
            return carry

        lax.fori_loop(0, 4, field_rows, 0)
        if with_flags:

            def flag_rows(part, carry):
                for place, source in enumerate((flags_low, flags, flags_high)):
                    row_flags_low[place, part, plane] = source[part, plane, 7 : 7 + rows]
                    row_flags_high[place, part, plane] = source[part, plane, 9 : 9 + rows]
                return carry

            lax.fori_loop(0, 2, flag_rows, 0)
            for field in range(2):
                far_low[field, plane] = fields[field + 1, plane, 6 : 6 + rows]
                far_high[field, plane] = fields[field + 1, plane, 10 : 10 + rows]
            far_flags[plane] = flags[0, plane, 6 : 6 + rows]

    def force_on(plane, choose, emit):
        def body(index, carry):
            start = pl.multiple_of(index * BAND, 8)
            own_rows = pl.ds(start + 8, BAND)
            own = [fields[field, plane, own_rows] for field in range(4)]
            force = [jnp.zeros((BAND, cells), jnp.float32) for _ in range(3)]
            for number, (step_x, step_y, step_z, weight) in enumerate(table):
                for sign in (1, -1):
                    if not choose(step_x, sign):
                        continue
                    step = (sign * step_x, sign * step_y, sign * step_z)
                    there = plane + step[0]

                    def load(plain, low, high, less, more, far_less, far_more, first):
                        if step[1] == -2:
                            return far_less(first, there)
                        if step[1] == 2:
                            return far_more(first, there)
                        if step[1] != 0:
                            shifted = less if step[1] < 0 else more
                            return shifted[step[2] + 1, first, there, pl.ds(start, BAND)]
                        if step[2] == 0:
                            return plain[first, there, own_rows]
                        if step[2] == 1:
                            return high[first, there, own_rows]
                        if step[2] == -1:
                            return low[first, there, own_rows]
                        return moved_along_cells(plain[first, there, own_rows], step[2])

                    def field_at(first):
                        return load(
                            fields, fields_low, fields_high, rows_low, rows_high,
                            lambda f, p: far_low[f - 1, p, pl.ds(start, BAND)],
                            lambda f, p: far_high[f - 1, p, pl.ds(start, BAND)],
                            first,
                        )

                    along = None
                    for component in range(3):
                        if step[component] == 0:
                            continue
                        part = field_at(PLACE[component])
                        part = part - own[PLACE[component]]
                        if step[component] < 0:
                            part = -part
                        along = part if along is None else along + part
                    size = 2.0 if max(abs(s) for s in step) == 2 else 1.0
                    scale = field_at(1)
                    if sign == 1:
                        source = flags[number // 8, plane, own_rows]
                    else:
                        source = load(
                            flags, flags_low, flags_high, row_flags_low, row_flags_high,
                            lambda f, p: far_flags[p, pl.ds(start, BAND)], None, number // 8,
                        )
                    factor = (weight * size * size) * scale * along
                    factor = jnp.where(
                        jnp.bitwise_and(source, 1 << (number % 8)) == 0, factor, 0.0
                    )
                    for component in range(3):
                        if step[component] > 0:
                            force[component] = force[component] + factor
                        elif step[component] < 0:
                            force[component] = force[component] - factor
            emit(pl.ds(start, BAND), [own[1] * total for total in force])
            return carry

        lax.fori_loop(0, rows // BAND, body, 0)

    def keep_partial(plane):
        def emit(where, force):
            for component in range(3):
                partial[plane, component, where] = force[component]
        return emit

    def finish(plane):
        def emit(where, force):
            for component in range(3):
                new = velocity[component, plane, where] + 0.1 * force[component]
                result[3 + component, plane, where] = new
                result[component, plane, where] = (
                    displacement[component, plane, where] + 0.1 * new
                )
        return emit

    ride_both(0)
    for copy in beside:
        copy.wait()
    for plane in range(planes):
        shift_plane(plane, True)
    ride_both(1)
    force_on(0, lambda step_x, sign: sign == 1 or step_x == 0, keep_partial(0))
    force_on(1, lambda step_x, sign: sign == 1 or step_x <= 1, keep_partial(1))
    ride_both(2)

    @pl.when(has_low)
    def _():
        for copy in below:
            copy.wait_send()

    @pl.when(has_high)
    def _():
        for copy in below:
            copy.wait_recv()

    shift_plane(planes, False)

    def keep_back(where, force):
        for component in range(3):
            back[component, where] = force[component]

    def keep_far(where, force):
        back[3, where] = force[0]

    force_on(planes, lambda step_x, sign: sign == -1 and step_x > 0, keep_back)

    @pl.when(has_high)
    def _():
        above[0].start()

    force_on(planes + 1, lambda step_x, sign: sign == -1 and step_x == 2, keep_far)

    @pl.when(has_high)
    def _():
        above[1].start()

    for plane in range(2, planes):
        force_on(plane, lambda step_x, sign: True, finish(plane))

    @pl.when(has_low)
    def _():
        above[0].wait_recv()

    for component in range(3):
        total = partial[0, component] + returned[component]
        ready_velocity[component] = velocity[component, 0] + 0.1 * total
    ride_both(3)

    @pl.when(has_low)
    def _():
        above[1].wait_recv()

    @pl.when(has_high)
    def _():
        for copy in above:
            copy.wait_send()

    for component in range(3):
        total = partial[1, component]
        if component == 0:
            total = total + returned[3]
        new = velocity[component, 1] + 0.1 * total
        result[3 + component, 1] = new
        result[component, 1] = displacement[component, 1] + 0.1 * new
    for step in range(4, last + 1):
        ride_both(step)


def on_device(displacement, velocity, damage, broken, counts, bits):
    planes, rows, cells = damage.shape
    half = cells // 2
    slab = lax.axis_index("slab")
    steps = jnp.arange(ROUNDS)
    partner = jnp.bitwise_xor(slab, jnp.left_shift(jnp.int32(1), bits))
    taken = jnp.minimum(counts[slab], counts[partner, steps])
    rounds_of = jnp.sum(
        jnp.where(bits[None, :] == steps[:, None], steps[None, :], 0), axis=1
    ).astype(jnp.int32)
    vmem = pl.BlockSpec(memory_space=pltpu.VMEM)
    smem = pl.BlockSpec(memory_space=pltpu.SMEM)
    f32, i32 = jnp.float32, jnp.int32
    tall = rows + 16
    return pl.pallas_call(
        kernel,
        out_shape=jax.ShapeDtypeStruct((6, planes, rows, cells), f32),
        in_specs=[smem] * 3 + [vmem] * 4,
        out_specs=vmem,
        scratch_shapes=[
            pltpu.VMEM((4, planes + 2, tall, cells), f32),
            pltpu.VMEM((2, planes, tall, cells), i32),
            pltpu.VMEM((4, planes + 1, tall, cells), f32),
            pltpu.VMEM((4, planes + 1, tall, cells), f32),
            pltpu.VMEM((2, planes, tall, cells), i32),
            pltpu.VMEM((2, planes, tall, cells), i32),
            pltpu.VMEM((3, 4, planes + 1, rows, cells), f32),
            pltpu.VMEM((3, 4, planes + 1, rows, cells), f32),
            pltpu.VMEM((3, 2, planes, rows, cells), i32),
            pltpu.VMEM((3, 2, planes, rows, cells), i32),
            pltpu.VMEM((2, planes, rows, cells), f32),
            pltpu.VMEM((2, planes, rows, cells), f32),
            pltpu.VMEM((planes, rows, cells), i32),
            pltpu.VMEM((2, 3, rows, cells), f32),
            pltpu.VMEM((4, rows, cells), f32),
            pltpu.VMEM((4, rows, cells), f32),
            pltpu.VMEM((2, ROUNDS, rows, half), f32),
            pltpu.VMEM((3, rows, cells), f32),
            pltpu.VMEM((3, rows, cells), f32),
        ]
        + [pltpu.VMEM((ROUNDS, rows, half), f32)] * 8
        + [
            pltpu.SemaphoreType.DMA((2,)),
            pltpu.SemaphoreType.DMA((2,)),
            pltpu.SemaphoreType.DMA((3,)),
            pltpu.SemaphoreType.DMA((3,)),
            pltpu.SemaphoreType.DMA((2,)),
            pltpu.SemaphoreType.DMA((2,)),
            pltpu.SemaphoreType.DMA((2, 2, ROUNDS)),
            pltpu.SemaphoreType.DMA((2, 2, ROUNDS)),
        ],
        compiler_params=pltpu.CompilerParams(
            collective_id=0, has_side_effects=True, vmem_limit_bytes=48 * 1024 * 1024
        ),
    )(taken, bits, rounds_of, displacement, velocity, damage, broken)


def solution(mesh):
    return jax.shard_map(
        on_device,
        mesh=mesh,
        in_specs=(
            P(None, "slab", "col", None),
            P(None, "slab", "col", None),
            P("slab", "col", None),
            P(None, "slab", "col", None),
            P(),
            P(),
        ),
        out_specs=P(None, "slab", "col", None),
        check_vma=False,
    )
```

time: 111 us -> 67.8 us (0.61)
  Pallas kernels: 0 us -> 58.4 us
  waiting for transfers between devices: 55.7 us -> 0 us
  other arithmetic: 23 us -> 1.44 us
  starting transfers between devices: 17.7 us -> 0 us
  between operations: 10.7 us -> 0.02 us
  local copies, waits for them, and re-layouts: 4.4 us -> 7.57 us
    pallas_call x0 -> x1, Pallas kernels: none -> 58.4 us  [on_device(): pl.pallas_call(kernel, out_shape=jax.ShapeDtypeStruct((6, planes, rows, c...]
    ppermute x9 -> x0, waiting for transfers between devices: 55.7 us -> none  [the longest x5 43.4 us: from_partner(): return lax.ppermute(block, axis, route)]
    ppermute x9 -> x0, starting transfers between devices: 17.7 us -> none  [the longest x5 9 us: from_partner(): return lax.ppermute(block, axis, route)]
    add x3 -> x0, other arithmetic: 9.17 us -> none  [the longest x1 5.45 us: on_device(): reaction = reaction + placed]
    unnamed x94 -> x13, local copies, waits for them, and re-layouts: 1.85 us -> 6.74 us
    mul x14 -> x0, other arithmetic: 4.31 us -> none  [bond_term(): return jnp.stack([factor * step_x, factor * step_y, factor * step_z])]
    scatter x3 -> x0, other arithmetic: 3.35 us -> none  [on_device(): columns = columns.at[:, :capacity].set(leading)]
    neg x9 -> x0, other arithmetic: 2.3 us -> none  [on_device(): -term]
  transfers between devices with their start and end apart: 9 -> 0, of which waited for: 7 -> 0; matrix products, arithmetic and copies ran while one was open for 6% -> 0% of each run, Pallas kernels for 0% -> 0%
where the time goes in v1:
time: 67.8 us; the launch traced here: 67.4 us
  Pallas kernels  58.4 us (86%)
  local copies, waits for them, and re-layouts  7.57 us (11%)
  other arithmetic  1.44 us (2%)
    pallas_call x1, Pallas kernels, on_device(): pl.pallas_call(kernel, out_shape=jax.ShapeDtypeStruct((6, planes, rows, c...  58.4 us
    unnamed x13, local copies, waits for them, and re-layouts  6.74 us

profile of v1, /device:TPU:0, one launch (start us, length us, event | category | flops | bytes accessed | tf_op | source)
XLA Modules:
  0.0 67.4 jit_solution(4287397159633357192)
XLA Ops:
  0.0 0.0 copy-start
  0.0 0.7 %copy-done = s32[16,4]{0,1:T(4,128)S(1)} copy-done((s32[16,4]{0,1:T(4,128)S(1)}, s32[16,4]{0,1:T(4,128)}, u32[]{:S(2)}) %copy-start) | copy-done | bytes 280
  0.7 0.2 dynamic-slice_reduce_fusion
  0.9 0.7 fusion.4
  1.5 0.6 gather_fusion
  2.2 0.8 %select_reduce_fusion.rounds_of = s32[4]{0:T(128)S(1)} fusion(s32[4]{0:T(128)} %bits.1), kind=kLoop, calls=%fused_computation.2 | loop fusion | flops 44 | bytes 32 | tf_op jit(solution)/shard_map/reduce_sum | solution.py:390
  3.0 0.0 copy-start.1
  3.0 1.1 %copy-done.1 = f32[3,4,64,256]{3,2,1,0:T(8,128)S(1)} copy-done((f32[3,4,64,256]{3,2,1,0:T(8,128)S(1)}, f32[3,4,64,256]{3,2,1,0:T(8,128)}, u32[]{:S(2)}) %copy-start.1) | copy-done | bytes 786456
  4.1 0.0 copy-start.2
  4.1 1.1 %copy-done.2 = f32[3,4,64,256]{3,2,1,0:T(8,128)S(1)} copy-done((f32[3,4,64,256]{3,2,1,0:T(8,128)S(1)}, f32[3,4,64,256]{3,2,1,0:T(8,128)}, u32[]{:S(2)}) %copy-start.2) | copy-done | bytes 786456
  5.2 0.0 copy-start.3
  5.2 1.0 %copy-done.3 = s32[2,4,64,256]{3,2,1,0:T(8,128)S(1)} copy-done((s32[2,4,64,256]{3,2,1,0:T(8,128)S(1)}, s32[2,4,64,256]{3,2,1,0:T(8,128)}, u32[]{:S(2)}) %copy-start.3) | copy-done | bytes 524312
  6.3 0.0 copy-start.4
  6.3 0.9 %copy-done.4 = f32[4,64,256]{2,1,0:T(8,128)S(1)} copy-done((f32[4,64,256]{2,1,0:T(8,128)S(1)}, f32[4,64,256]{2,1,0:T(8,128)}, u32[]{:S(2)}) %copy-start.4) | copy-done | bytes 262168
  7.2 0.0 copy-start.5
  7.2 0.7 copy-done.5
  7.9 58.4 %shard_map.64 = f32[6,4,64,256]{3,2,1,0:T(8,128)S(1)} custom-call(s32[4]{0:T(128)S(1)} %min.3.taken, s32[4]{0:T(128)S(1)} %copy-done.5, s32[4]{0:T(128)S(1)} %select_reduce_fusion.rounds_of, f32[3,4,64,256]{3,2,1,0:T(8,128)S(1)} %copy-done.1, f32[3,4,64,256]{3,2,1,0:T(8,128)S(1)} %copy-done.2, f32[4,64,256]{2,1,0:T(8,128)S(1)} %copy-done.4, ...), custom_call_target="tpu_custom_call" | custom-call | tf_op jit(solution)/shard_map/pallas_call | solution.py:397
  66.3 1.1 %copy.8 = f32[6,4,64,256]{3,2,1,0:T(8,128)} copy(f32[6,4,64,256]{3,2,1,0:T(8,128)S(1)} %shard_map.64) | data formatting | bytes 3145728
  (1 shorter events, 0.0 us)
Async XLA Ops:
  0.0 0.7 %copy-start = (s32[16,4]{0,1:T(4,128)S(1)}, s32[16,4]{0,1:T(4,128)}, u32[]{:S(2)}) copy-start(s32[16,4]{0,1:T(4,128)} %param.10) | copy-start | bytes 772
  3.0 1.1 %copy-start.1 = (f32[3,4,64,256]{3,2,1,0:T(8,128)S(1)}, f32[3,4,64,256]{3,2,1,0:T(8,128)}, u32[]{:S(2)}) copy-start(f32[3,4,64,256]{3,2,1,0:T(8,128)} %displacement.1) | copy-start | bytes 2359300
  4.1 1.1 %copy-start.2 = (f32[3,4,64,256]{3,2,1,0:T(8,128)S(1)}, f32[3,4,64,256]{3,2,1,0:T(8,128)}, u32[]{:S(2)}) copy-start(f32[3,4,64,256]{3,2,1,0:T(8,128)} %velocity.1) | copy-start | bytes 2359300
  5.2 1.0 %copy-start.3 = (s32[2,4,64,256]{3,2,1,0:T(8,128)S(1)}, s32[2,4,64,256]{3,2,1,0:T(8,128)}, u32[]{:S(2)}) copy-start(s32[2,4,64,256]{3,2,1,0:T(8,128)} %broken.1) | copy-start | bytes 1572868
  6.3 0.9 %copy-start.4 = (f32[4,64,256]{2,1,0:T(8,128)S(1)}, f32[4,64,256]{2,1,0:T(8,128)}, u32[]{:S(2)}) copy-start(f32[4,64,256]{2,1,0:T(8,128)} %damage.1) | copy-start | bytes 786436
  7.2 0.7 copy-start.5

commit v2 on v1

--- a/solution.py
+++ b/solution.py
@@ -12,6 +12,8 @@
 PLACE = (0, 2, 3)
 BAND = 16
 ROUNDS = 4
+PIPES = 4
+PARTS = 4
 
 
 def bond_table():
@@ -35,14 +37,16 @@
 
 
 def kernel(
-    taken, bits, rounds_of, displacement, velocity, damage, broken, result,
-    fields, flags, fields_low, fields_high, flags_low, flags_high,
+    counts, bits, displacement, velocity_in, damage, broken, result,
+    fields, flags, velocity, fields_low, fields_high, flags_low, flags_high,
     rows_low, rows_high, row_flags_low, row_flags_high, far_low, far_high, far_flags,
-    partial, back, returned, stage, arrived, ready_velocity,
-    in00, in01, in10, in11, out00, out01, out10, out11,
-    col_send, col_recv, down_send, down_recv, back_send, back_recv,
-    ride_send, ride_recv,
+    partial, back, returned, stage, arrived, ready_velocity, *rest,
 ):
+    buffers, rest = rest[: 4 * PIPES], rest[4 * PIPES :]
+    (
+        col_send, col_recv, down_send, down_recv, back_send, back_recv,
+        ride_send, ride_recv, load_done,
+    ) = rest
     planes, rows, cells = damage.shape
     half = cells // 2
     slabs = lax.axis_size("slab")
@@ -52,13 +56,24 @@
     has_low = slab > 0
     has_high = slab < slabs - 1
     table = bond_table()
-    incoming = ((in00, in01), (in10, in11))
-    outgoing = ((out00, out01), (out10, out11))
-
-    for component in range(3):
-        fields[PLACE[component], 0:planes, 8 : 8 + rows] = displacement[component]
-    fields[1, 0:planes, 8 : 8 + rows] = damage[...]
-    flags[:, :, 8 : 8 + rows] = broken[...]
+    incoming = [buffers[2 * pipe : 2 * pipe + 2] for pipe in range(PIPES)]
+    outgoing = [buffers[2 * (PIPES + pipe) : 2 * (PIPES + pipe) + 2] for pipe in range(PIPES)]
+
+    inner = pl.ds(8, rows)
+    loads = [
+        pltpu.make_async_copy(
+            displacement.at[component], fields.at[PLACE[component], 0:planes, inner],
+            load_done.at[component],
+        )
+        for component in range(3)
+    ]
+    loads.append(
+        pltpu.make_async_copy(damage, fields.at[1, 0:planes, inner], load_done.at[3])
+    )
+    load_flags = pltpu.make_async_copy(broken, flags.at[:, :, inner], load_done.at[4])
+    load_velocity = pltpu.make_async_copy(velocity_in, velocity, load_done.at[5])
+    for copy in loads + [load_flags, load_velocity]:
+        copy.start()
     fields[:, 0:planes, 0:8] = jnp.zeros((4, planes, 8, cells), jnp.float32)
     fields[:, 0:planes, 8 + rows : 16 + rows] = jnp.zeros((4, planes, 8, cells), jnp.float32)
     fields[:, planes : planes + 2] = jnp.zeros((4, 2, rows + 16, cells), jnp.float32)
@@ -72,6 +87,18 @@
         weight = 1 << bit
         partners.append(slab + weight - 2 * weight * ((slab // weight) % 2))
 
+    taken, rounds_of = [], []
+    for number in range(ROUNDS):
+        partner = partners[0]
+        for bit in range(1, ROUNDS):
+            partner = jnp.where(bits[number] == bit, partners[bit], partner)
+        taken.append(jnp.minimum(counts[slab, number], counts[partner, number]))
+    for bit in range(ROUNDS):
+        place = jnp.int32(0)
+        for number in range(1, ROUNDS):
+            place = jnp.where(bits[number] == bit, number, place)
+        rounds_of.append(place)
+
     barrier = pltpu.get_barrier_semaphore()
 
     def greet(to_slab, to_col):
@@ -109,7 +136,6 @@
         remote(flags.at[:, :, rim], flags.at[:, :, ghost],
                col_send.at[1], col_recv.at[1], slab, other),
     ]
-    inner = pl.ds(8, rows)
     below = [
         remote(fields.at[:, 0, inner], fields.at[:, planes, inner],
                down_send.at[0], down_recv.at[0], slab - 1, col),
@@ -123,15 +149,19 @@
         remote(back.at[3], returned.at[3], back_send.at[1], back_recv.at[1], slab + 1, col),
     ]
 
+    for copy in loads:
+        copy.wait()
+
     @pl.when(has_low)
     def _():
         for copy in below:
             copy.start()
 
-    for copy in beside:
-        copy.start()
-
-    column = lax.broadcasted_iota(jnp.int32, (rows, half), 0)
+    beside[0].start()
+    load_flags.wait()
+    beside[1].start()
+
+    column = lax.broadcasted_iota(jnp.int32, (3, 8, half), 1)
 
     def rides(pipe, step):
         parity = step % 2
@@ -142,32 +172,43 @@
             for bit in range(ROUNDS)
         ]
 
-    last = 6 + ROUNDS - 1
+    last = 2 * PARTS + ROUNDS - 1
 
     def ride(pipe, step):
-        lanes = slice(pipe * half, (pipe + 1) * half)
+        def spot(item):
+            part = item % PARTS
+            first = pipe * (rows // PIPES) + (part // 2) * 8
+            return slice(first, first + 8), slice(part % 2 * half, (part % 2 + 1) * half)
+
         if step > 0:
             for copy in rides(pipe, step - 1):
                 copy.wait_recv()
             source = incoming[pipe][(step - 1) % 2]
             for number in reversed(range(ROUNDS)):
+                item = step - 1 - number
+                if not 0 <= item < 2 * PARTS:
+                    continue
+                where, lanes = spot(item)
                 new = jnp.where(
-                    column < taken[number], source[bits[number]], stage[pipe, number]
+                    column < taken[number] - where.start,
+                    source[bits[number]], stage[pipe, number],
                 )
                 if number < ROUNDS - 1:
                     stage[pipe, number + 1] = new
-                elif step >= ROUNDS:
-                    item = step - ROUNDS
-                    if item < 3:
-                        arrived[item, :, lanes] = new
-                    else:
-                        result[item, 0, :, lanes] = new
-                        result[item - 3, 0, :, lanes] = arrived[item - 3, :, lanes] + 0.1 * new
+                elif item < PARTS:
+                    arrived[:, where, lanes] = new
+                else:
+                    result[3:6, 0, where, lanes] = new
+                    result[0:3, 0, where, lanes] = arrived[:, where, lanes] + 0.1 * new
         if step < last:
-            if step < 3:
-                stage[pipe, 0] = displacement[step, 0, :, lanes]
-            elif step < 6:
-                stage[pipe, 0] = ready_velocity[step - 3, :, lanes]
+            if step < 2 * PARTS:
+                where, lanes = spot(step)
+                if step < PARTS:
+                    tall = slice(where.start + 8, where.stop + 8)
+                    for component in range(3):
+                        stage[pipe, 0, component] = fields[PLACE[component], 0, tall, lanes]
+                else:
+                    stage[pipe, 0] = ready_velocity[:, where, lanes]
             if step >= 2:
                 for copy in rides(pipe, step - 2):
                     copy.wait_send()
@@ -182,24 +223,19 @@
                     copy.wait_send()
 
     def ride_both(step):
-        for pipe in range(2):
+        for pipe in range(PIPES):
             ride(pipe, step)
 
     def shift_plane(plane, with_flags):
-        def body(index, carry):
-            here = pl.ds(pl.multiple_of(index * 8, 8), 8)
-            for field in range(4):
-                value = fields[field, plane, here]
-                fields_low[field, plane, here] = moved_along_cells(value, -1)
-                fields_high[field, plane, here] = moved_along_cells(value, 1)
-            if with_flags:
-                for part in range(2):
-                    value = flags[part, plane, here]
-                    flags_low[part, plane, here] = moved_along_cells(value, -1)
-                    flags_high[part, plane, here] = moved_along_cells(value, 1)
-            return carry
-
-        lax.fori_loop(0, (rows + 16) // 8, body, 0)
+        for field in range(4):
+            value = fields[field, plane]
+            fields_low[field, plane] = moved_along_cells(value, -1)
+            fields_high[field, plane] = moved_along_cells(value, 1)
+        if with_flags:
+            for part in range(2):
+                value = flags[part, plane]
+                flags_low[part, plane] = moved_along_cells(value, -1)
+                flags_high[part, plane] = moved_along_cells(value, 1)
 
         def field_rows(field, carry):
             for place, source in enumerate((fields_low, fields, fields_high)):
@@ -303,19 +339,24 @@
                 new = velocity[component, plane, where] + 0.1 * force[component]
                 result[3 + component, plane, where] = new
                 result[component, plane, where] = (
-                    displacement[component, plane, where] + 0.1 * new
+                    fields[PLACE[component], plane, pl.ds(where.start + 8, BAND)] + 0.1 * new
                 )
         return emit
 
     ride_both(0)
     for copy in beside:
         copy.wait()
-    for plane in range(planes):
+    ride_both(1)
+
+    def shift_own(plane, carry):
         shift_plane(plane, True)
-    ride_both(1)
+        return carry
+
+    lax.fori_loop(0, planes, shift_own, 0)
+    ride_both(2)
     force_on(0, lambda step_x, sign: sign == 1 or step_x == 0, keep_partial(0))
     force_on(1, lambda step_x, sign: sign == 1 or step_x <= 1, keep_partial(1))
-    ride_both(2)
+    ride_both(3)
 
     @pl.when(has_low)
     def _():
@@ -348,6 +389,7 @@
     def _():
         above[1].start()
 
+    load_velocity.wait()
     for plane in range(2, planes):
         force_on(plane, lambda step_x, sign: True, finish(plane))
 
@@ -358,7 +400,7 @@
     for component in range(3):
         total = partial[0, component] + returned[component]
         ready_velocity[component] = velocity[component, 0] + 0.1 * total
-    ride_both(3)
+    ride_both(PARTS)
 
     @pl.when(has_low)
     def _():
@@ -375,33 +417,28 @@
             total = total + returned[3]
         new = velocity[component, 1] + 0.1 * total
         result[3 + component, 1] = new
-        result[component, 1] = displacement[component, 1] + 0.1 * new
-    for step in range(4, last + 1):
+        result[component, 1] = fields[PLACE[component], 1, 8 : 8 + rows] + 0.1 * new
+    for step in range(PARTS + 1, last + 1):
         ride_both(step)
 
 
 def on_device(displacement, velocity, damage, broken, counts, bits):
     planes, rows, cells = damage.shape
     half = cells // 2
-    slab = lax.axis_index("slab")
-    steps = jnp.arange(ROUNDS)
-    partner = jnp.bitwise_xor(slab, jnp.left_shift(jnp.int32(1), bits))
-    taken = jnp.minimum(counts[slab], counts[partner, steps])
-    rounds_of = jnp.sum(
-        jnp.where(bits[None, :] == steps[:, None], steps[None, :], 0), axis=1
-    ).astype(jnp.int32)
     vmem = pl.BlockSpec(memory_space=pltpu.VMEM)
     smem = pl.BlockSpec(memory_space=pltpu.SMEM)
+    hbm = pl.BlockSpec(memory_space=pltpu.HBM)
     f32, i32 = jnp.float32, jnp.int32
     tall = rows + 16
     return pl.pallas_call(
         kernel,
         out_shape=jax.ShapeDtypeStruct((6, planes, rows, cells), f32),
-        in_specs=[smem] * 3 + [vmem] * 4,
+        in_specs=[smem] * 2 + [hbm] * 4,
         out_specs=vmem,
         scratch_shapes=[
             pltpu.VMEM((4, planes + 2, tall, cells), f32),
             pltpu.VMEM((2, planes, tall, cells), i32),
+            pltpu.VMEM((3, planes, rows, cells), f32),
             pltpu.VMEM((4, planes + 1, tall, cells), f32),
             pltpu.VMEM((4, planes + 1, tall, cells), f32),
             pltpu.VMEM((2, planes, tall, cells), i32),
@@ -416,11 +453,11 @@
             pltpu.VMEM((2, 3, rows, cells), f32),
             pltpu.VMEM((4, rows, cells), f32),
             pltpu.VMEM((4, rows, cells), f32),
-            pltpu.VMEM((2, ROUNDS, rows, half), f32),
+            pltpu.VMEM((PIPES, ROUNDS, 3, 8, half), f32),
             pltpu.VMEM((3, rows, cells), f32),
             pltpu.VMEM((3, rows, cells), f32),
         ]
-        + [pltpu.VMEM((ROUNDS, rows, half), f32)] * 8
+        + [pltpu.VMEM((ROUNDS, 3, 8, half), f32)] * (4 * PIPES)
         + [
             pltpu.SemaphoreType.DMA((2,)),
             pltpu.SemaphoreType.DMA((2,)),
@@ -428,13 +465,14 @@
             pltpu.SemaphoreType.DMA((3,)),
             pltpu.SemaphoreType.DMA((2,)),
             pltpu.SemaphoreType.DMA((2,)),
-            pltpu.SemaphoreType.DMA((2, 2, ROUNDS)),
-            pltpu.SemaphoreType.DMA((2, 2, ROUNDS)),
+            pltpu.SemaphoreType.DMA((PIPES, 2, ROUNDS)),
+            pltpu.SemaphoreType.DMA((PIPES, 2, ROUNDS)),
+            pltpu.SemaphoreType.DMA((6,)),
         ],
         compiler_params=pltpu.CompilerParams(
-            collective_id=0, has_side_effects=True, vmem_limit_bytes=48 * 1024 * 1024
+            collective_id=0, has_side_effects=True, vmem_limit_bytes=62 * 1024 * 1024
         ),
-    )(taken, bits, rounds_of, displacement, velocity, damage, broken)
+    )(counts, bits, displacement, velocity, damage, broken)
 
 
 def solution(mesh):

time: 67.8 us -> 65.6 us (0.968)
  local copies, waits for them, and re-layouts: 7.57 us -> 4.06 us
  Pallas kernels: 58.4 us -> 61.3 us
  other arithmetic: 1.44 us -> 0 us
    pallas_call x1, Pallas kernels: 58.4 us -> 61.3 us  [on_device(): pl.pallas_call(kernel, out_shape=jax.ShapeDtypeStruct((6, planes, rows, c...]
    unnamed x13 -> x2, local copies, waits for them, and re-layouts: 6.74 us -> 4.06 us
    reduce_sum x1 -> x0, other arithmetic: 0.77 us -> none  [on_device(): jnp.sum(jnp.where(bits[None, :] == steps[:, None], steps[None, :], 0), ax...]
where the time goes in v2:
time: 65.6 us; the launch traced here: 65.3 us
  Pallas kernels  61.3 us (93%)
  local copies, waits for them, and re-layouts  4.06 us (6%)
    pallas_call x1, Pallas kernels, on_device(): pl.pallas_call(kernel, out_shape=jax.ShapeDtypeStruct((6, planes, rows, c...  61.3 us
    unnamed x2, local copies, waits for them, and re-layouts  4.06 us

profile of v2, /device:TPU:0, one launch (start us, length us, event | category | flops | bytes accessed | tf_op | source)
XLA Modules:
  0.0 65.3 jit_solution(17380968327743661569)
XLA Ops:
  0.0 1.4 %copy.7.counts = s32[16,4]{1,0:T(8,128)} copy(s32[16,4]{0,1:T(4,128)} %param.10) | data formatting | bytes 512 | tf_op args[4]
  1.4 61.3 %shard_map.64 = f32[6,4,64,256]{3,2,1,0:T(8,128)} custom-call(s32[16,4]{1,0:T(8,128)} %copy.7.counts, s32[4]{0:T(128)} %bits.1, f32[3,4,64,256]{3,2,1,0:T(8,128)} %displacement.1, f32[3,4,64,256]{3,2,1,0:T(8,128)} %velocity_in.1, f32[4,64,256]{2,1,0:T(8,128)} %damage.1, s32[2,4,64,256]{3,2,1,0:T(8,128)} %broken.1), custom_call_target="tpu_custom_call" | custom-call | tf_op jit(solution)/shard_map/pallas_call | solution.py:433
  62.6 2.7 %copy.9 = f32[6,4,64,256]{3,2,1,0:T(8,128)} copy(f32[6,4,64,256]{3,2,1,0:T(8,128)} %shard_map.64) | data formatting | bytes 3145728

commit v3 on v2

--- a/solution.py
+++ b/solution.py
@@ -92,7 +92,7 @@
         partner = partners[0]
         for bit in range(1, ROUNDS):
             partner = jnp.where(bits[number] == bit, partners[bit], partner)
-        taken.append(jnp.minimum(counts[slab, number], counts[partner, number]))
+        taken.append(jnp.minimum(counts[number, slab], counts[number, partner]))
     for bit in range(ROUNDS):
         place = jnp.int32(0)
         for number in range(1, ROUNDS):
@@ -154,7 +154,7 @@
 
     @pl.when(has_low)
     def _():
-        for copy in below:
+        for copy in below[0:2]:
             copy.start()
 
     beside[0].start()
@@ -258,7 +258,7 @@
                 far_high[field, plane] = fields[field + 1, plane, 10 : 10 + rows]
             far_flags[plane] = flags[0, plane, 6 : 6 + rows]
 
-    def force_on(plane, choose, emit):
+    def force_on(plane, choose, emit, first=0, stop=rows // BAND):
         def body(index, carry):
             start = pl.multiple_of(index * BAND, 8)
             own_rows = pl.ds(start + 8, BAND)
@@ -325,7 +325,7 @@
             emit(pl.ds(start, BAND), [own[1] * total for total in force])
             return carry
 
-        lax.fori_loop(0, rows // BAND, body, 0)
+        lax.fori_loop(first, stop, body, 0)
 
     def keep_partial(plane):
         def emit(where, force):
@@ -343,9 +343,21 @@
                 )
         return emit
 
+    def keep_back(where, force):
+        for component in range(3):
+            back[component, where] = force[component]
+
+    def keep_far(where, force):
+        back[3, where] = force[0]
+
     ride_both(0)
     for copy in beside:
         copy.wait()
+
+    @pl.when(has_low)
+    def _():
+        below[2].start()
+
     ride_both(1)
 
     def shift_own(plane, carry):
@@ -355,43 +367,28 @@
     lax.fori_loop(0, planes, shift_own, 0)
     ride_both(2)
     force_on(0, lambda step_x, sign: sign == 1 or step_x == 0, keep_partial(0))
+
+    @pl.when(has_high)
+    def _():
+        for copy in below[0:2]:
+            copy.wait_recv()
+
+    force_on(planes, lambda step_x, sign: sign == -1 and step_x > 0, keep_back)
+
+    @pl.when(has_high)
+    def _():
+        above[0].start()
+        below[2].wait_recv()
+
+    force_on(planes + 1, lambda step_x, sign: sign == -1 and step_x == 2, keep_far)
+
+    @pl.when(has_high)
+    def _():
+        above[1].start()
+
+    ride_both(3)
+    load_velocity.wait()
     force_on(1, lambda step_x, sign: sign == 1 or step_x <= 1, keep_partial(1))
-    ride_both(3)
-
-    @pl.when(has_low)
-    def _():
-        for copy in below:
-            copy.wait_send()
-
-    @pl.when(has_high)
-    def _():
-        for copy in below:
-            copy.wait_recv()
-
-    shift_plane(planes, False)
-
-    def keep_back(where, force):
-        for component in range(3):
-            back[component, where] = force[component]
-
-    def keep_far(where, force):
-        back[3, where] = force[0]
-
-    force_on(planes, lambda step_x, sign: sign == -1 and step_x > 0, keep_back)
-
-    @pl.when(has_high)
-    def _():
-        above[0].start()
-
-    force_on(planes + 1, lambda step_x, sign: sign == -1 and step_x == 2, keep_far)
-
-    @pl.when(has_high)
-    def _():
-        above[1].start()
-
-    load_velocity.wait()
-    for plane in range(2, planes):
-        force_on(plane, lambda step_x, sign: True, finish(plane))
 
     @pl.when(has_low)
     def _():
@@ -400,11 +397,13 @@
     for component in range(3):
         total = partial[0, component] + returned[component]
         ready_velocity[component] = velocity[component, 0] + 0.1 * total
-    ride_both(PARTS)
+    ride_both(4)
 
     @pl.when(has_low)
     def _():
         above[1].wait_recv()
+        for copy in below:
+            copy.wait_send()
 
     @pl.when(has_high)
     def _():
@@ -418,7 +417,20 @@
         new = velocity[component, 1] + 0.1 * total
         result[3 + component, 1] = new
         result[component, 1] = fields[PLACE[component], 1, 8 : 8 + rows] + 0.1 * new
-    for step in range(PARTS + 1, last + 1):
+    ride_both(5)
+    bands = rows // BAND
+    step = 6
+    for plane in range(2, planes):
+        if plane == planes - 1:
+            shift_plane(planes, False)
+        for part in range(2):
+            force_on(
+                plane, lambda step_x, sign: True, finish(plane),
+                part * bands // 2, (part + 1) * bands // 2,
+            )
+            ride_both(step)
+            step += 1
+    for step in range(step, last + 1):
         ride_both(step)
 
 
@@ -470,9 +482,9 @@
             pltpu.SemaphoreType.DMA((6,)),
         ],
         compiler_params=pltpu.CompilerParams(
-            collective_id=0, has_side_effects=True, vmem_limit_bytes=62 * 1024 * 1024
+            collective_id=0, has_side_effects=True, vmem_limit_bytes=60 * 1024 * 1024
         ),
-    )(counts, bits, displacement, velocity, damage, broken)
+    )(counts.T, bits, displacement, velocity, damage, broken)
 
 
 def solution(mesh):

time: 65.6 us -> 61.1 us (0.931)
  Pallas kernels: 61.3 us -> 58.2 us
  local copies, waits for them, and re-layouts: 4.06 us -> 2.7 us
    pallas_call x1, Pallas kernels: 61.3 us -> 58.2 us  [on_device(): pl.pallas_call(kernel, out_shape=jax.ShapeDtypeStruct((6, planes, rows, c...]
    unnamed x2 -> x1, local copies, waits for them, and re-layouts: 4.06 us -> 2.7 us
where the time goes in v3:
time: 61.1 us; the launch traced here: 60.9 us
  Pallas kernels  58.2 us (95%)
  local copies, waits for them, and re-layouts  2.7 us (4%)
    pallas_call x1, Pallas kernels, on_device(): pl.pallas_call(kernel, out_shape=jax.ShapeDtypeStruct((6, planes, rows, c...  58.2 us
    unnamed x1, local copies, waits for them, and re-layouts  2.7 us

profile of v3, /device:TPU:0, one launch (start us, length us, event | category | flops | bytes accessed | tf_op | source)
XLA Modules:
  0.0 60.9 jit_solution(10834115932822960118)
XLA Ops:
  0.0 58.2 %shard_map.64 = f32[6,4,64,256]{3,2,1,0:T(8,128)} custom-call(s32[4,16]{1,0:T(4,128)} %bitcast.1, s32[4]{0:T(128)} %bits.1, f32[3,4,64,256]{3,2,1,0:T(8,128)} %displacement.1, f32[3,4,64,256]{3,2,1,0:T(8,128)} %velocity_in.1, f32[4,64,256]{2,1,0:T(8,128)} %damage.1, s32[2,4,64,256]{3,2,1,0:T(8,128)} %broken.1), custom_call_target="tpu_custom_call" | custom-call | tf_op jit(solution)/shard_map/pallas_call | solution.py:445
  58.2 2.7 %copy.8 = f32[6,4,64,256]{3,2,1,0:T(8,128)} copy(f32[6,4,64,256]{3,2,1,0:T(8,128)} %shard_map.64) | data formatting | bytes 3145728

commit v4 on v3

--- a/solution.py
+++ b/solution.py
@@ -12,7 +12,7 @@
 PLACE = (0, 2, 3)
 BAND = 16
 ROUNDS = 4
-PIPES = 4
+PIPES = 2
 PARTS = 4
 
 
@@ -48,7 +48,6 @@
         ride_send, ride_recv, load_done,
     ) = rest
     planes, rows, cells = damage.shape
-    half = cells // 2
     slabs = lax.axis_size("slab")
     slab = lax.axis_index("slab")
     col = lax.axis_index("col")
@@ -161,7 +160,7 @@
     load_flags.wait()
     beside[1].start()
 
-    column = lax.broadcasted_iota(jnp.int32, (3, 8, half), 1)
+    column = lax.broadcasted_iota(jnp.int32, (3, 8, cells), 1)
 
     def rides(pipe, step):
         parity = step % 2
@@ -177,8 +176,8 @@
     def ride(pipe, step):
         def spot(item):
             part = item % PARTS
-            first = pipe * (rows // PIPES) + (part // 2) * 8
-            return slice(first, first + 8), slice(part % 2 * half, (part % 2 + 1) * half)
+            first = pipe * (rows // PIPES) + part * 8
+            return slice(first, first + 8), slice(0, cells)
 
         if step > 0:
             for copy in rides(pipe, step - 1):
@@ -436,7 +435,6 @@
 
 def on_device(displacement, velocity, damage, broken, counts, bits):
     planes, rows, cells = damage.shape
-    half = cells // 2
     vmem = pl.BlockSpec(memory_space=pltpu.VMEM)
     smem = pl.BlockSpec(memory_space=pltpu.SMEM)
     hbm = pl.BlockSpec(memory_space=pltpu.HBM)
@@ -465,11 +463,11 @@
             pltpu.VMEM((2, 3, rows, cells), f32),
             pltpu.VMEM((4, rows, cells), f32),
             pltpu.VMEM((4, rows, cells), f32),
-            pltpu.VMEM((PIPES, ROUNDS, 3, 8, half), f32),
+            pltpu.VMEM((PIPES, ROUNDS, 3, 8, cells), f32),
             pltpu.VMEM((3, rows, cells), f32),
             pltpu.VMEM((3, rows, cells), f32),
         ]
-        + [pltpu.VMEM((ROUNDS, 3, 8, half), f32)] * (4 * PIPES)
+        + [pltpu.VMEM((ROUNDS, 3, 8, cells), f32)] * (4 * PIPES)
         + [
             pltpu.SemaphoreType.DMA((2,)),
             pltpu.SemaphoreType.DMA((2,)),

time: 61.1 us -> 62.9 us (1.029)
  Pallas kernels: 58.2 us -> 59.9 us
    pallas_call x1, Pallas kernels: 58.2 us -> 59.9 us  [on_device(): pl.pallas_call(kernel, out_shape=jax.ShapeDtypeStruct((6, planes, rows, c...]
where the time goes in v4:
time: 62.9 us; the launch traced here: 62.6 us
  Pallas kernels  59.9 us (95%)
  local copies, waits for them, and re-layouts  2.7 us (4%)
    pallas_call x1, Pallas kernels, on_device(): pl.pallas_call(kernel, out_shape=jax.ShapeDtypeStruct((6, planes, rows, c...  59.9 us
    unnamed x1, local copies, waits for them, and re-layouts  2.7 us

profile of v4, /device:TPU:0, one launch (start us, length us, event | category | flops | bytes accessed | tf_op | source)
XLA Modules:
  0.0 62.6 jit_solution(5267731519926863578)
XLA Ops:
  0.0 59.9 %shard_map.64 = f32[6,4,64,256]{3,2,1,0:T(8,128)} custom-call(s32[4,16]{1,0:T(4,128)} %bitcast.1, s32[4]{0:T(128)} %bits.1, f32[3,4,64,256]{3,2,1,0:T(8,128)} %displacement.1, f32[3,4,64,256]{3,2,1,0:T(8,128)} %velocity_in.1, f32[4,64,256]{2,1,0:T(8,128)} %damage.1, s32[2,4,64,256]{3,2,1,0:T(8,128)} %broken.1), custom_call_target="tpu_custom_call" | custom-call | tf_op jit(solution)/shard_map/pallas_call | solution.py:443
  59.9 2.7 %copy.8 = f32[6,4,64,256]{3,2,1,0:T(8,128)} copy(f32[6,4,64,256]{3,2,1,0:T(8,128)} %shard_map.64) | data formatting | bytes 3145728

commit v5 on v3

--- a/solution.py
+++ b/solution.py
@@ -419,19 +419,17 @@
         result[component, 1] = fields[PLACE[component], 1, 8 : 8 + rows] + 0.1 * new
     ride_both(5)
     bands = rows // BAND
-    step = 6
-    for plane in range(2, planes):
-        if plane == planes - 1:
-            shift_plane(planes, False)
-        for part in range(2):
-            force_on(
-                plane, lambda step_x, sign: True, finish(plane),
-                part * bands // 2, (part + 1) * bands // 2,
-            )
-            ride_both(step)
-            step += 1
-    for step in range(step, last + 1):
-        ride_both(step)
+    work = [(plane, band) for plane in range(2, planes) for band in range(bands)]
+    for step in range(6, last + 1):
+        for pipe in range(PIPES):
+            if pipe % 2 == 0 and work:
+                plane, band = work.pop(0)
+                if plane == planes - 1 and band == 0:
+                    shift_plane(planes, False)
+                force_on(plane, lambda step_x, sign: True, finish(plane), band, band + 1)
+            ride(pipe, step)
+    for plane, band in work:
+        force_on(plane, lambda step_x, sign: True, finish(plane), band, band + 1)
 
 
 def on_device(displacement, velocity, damage, broken, counts, bits):

time: 61.1 us -> 61.1 us (level)
  no operation moved by 1% of the time
where the time goes in v5:
time: 61.1 us; the launch traced here: 60.9 us
  Pallas kernels  58.2 us (95%)
  local copies, waits for them, and re-layouts  2.7 us (4%)
    pallas_call x1, Pallas kernels, on_device(): pl.pallas_call(kernel, out_shape=jax.ShapeDtypeStruct((6, planes, rows, c...  58.2 us
    unnamed x1, local copies, waits for them, and re-layouts  2.7 us

profile of v5, /device:TPU:0, one launch (start us, length us, event | category | flops | bytes accessed | tf_op | source)
XLA Modules:
  0.0 60.9 jit_solution(7172489587229904162)
XLA Ops:
  0.0 58.2 %shard_map.64 = f32[6,4,64,256]{3,2,1,0:T(8,128)} custom-call(s32[4,16]{1,0:T(4,128)} %bitcast.1, s32[4]{0:T(128)} %bits.1, f32[3,4,64,256]{3,2,1,0:T(8,128)} %displacement.1, f32[3,4,64,256]{3,2,1,0:T(8,128)} %velocity_in.1, f32[4,64,256]{2,1,0:T(8,128)} %damage.1, s32[2,4,64,256]{3,2,1,0:T(8,128)} %broken.1), custom_call_target="tpu_custom_call" | custom-call | tf_op jit(solution)/shard_map/pallas_call | solution.py:443
  58.2 2.7 %copy.8 = f32[6,4,64,256]{3,2,1,0:T(8,128)} copy(f32[6,4,64,256]{3,2,1,0:T(8,128)} %shard_map.64) | data formatting | bytes 3145728

commit v6 on v3

--- a/solution.py
+++ b/solution.py
@@ -37,15 +37,15 @@
 
 
 def kernel(
-    counts, bits, displacement, velocity_in, damage, broken, result,
-    fields, flags, velocity, fields_low, fields_high, flags_low, flags_high,
+    counts, bits, displacement, velocity_in, damage, broken, written,
+    result, fields, flags, velocity, fields_low, fields_high, flags_low, flags_high,
     rows_low, rows_high, row_flags_low, row_flags_high, far_low, far_high, far_flags,
     partial, back, returned, stage, arrived, ready_velocity, *rest,
 ):
     buffers, rest = rest[: 4 * PIPES], rest[4 * PIPES :]
     (
         col_send, col_recv, down_send, down_recv, back_send, back_recv,
-        ride_send, ride_recv, load_done,
+        ride_send, ride_recv, load_done, write_done,
     ) = rest
     planes, rows, cells = damage.shape
     half = cells // 2
@@ -173,6 +173,20 @@
         ]
 
     last = 2 * PARTS + ROUNDS - 1
+    share = rows // PIPES
+    writes = [
+        pltpu.make_async_copy(
+            result.at[:, 0, pl.ds(pipe * share, share)],
+            written.at[:, 0, pl.ds(pipe * share, share)], write_done.at[pipe],
+        )
+        for pipe in range(PIPES)
+    ]
+    writes += [
+        pltpu.make_async_copy(
+            result.at[:, plane], written.at[:, plane], write_done.at[PIPES + plane - 1]
+        )
+        for plane in range(1, planes)
+    ]
 
     def ride(pipe, step):
         def spot(item):
@@ -218,6 +232,7 @@
             for copy in rides(pipe, step):
                 copy.start()
         else:
+            writes[pipe].start()
             for back_step in (last - 2, last - 1):
                 for copy in rides(pipe, back_step):
                     copy.wait_send()
@@ -417,6 +432,7 @@
         new = velocity[component, 1] + 0.1 * total
         result[3 + component, 1] = new
         result[component, 1] = fields[PLACE[component], 1, 8 : 8 + rows] + 0.1 * new
+    writes[PIPES].start()
     ride_both(5)
     bands = rows // BAND
     step = 6
@@ -428,16 +444,19 @@
                 plane, lambda step_x, sign: True, finish(plane),
                 part * bands // 2, (part + 1) * bands // 2,
             )
+            if part == 1:
+                writes[PIPES + plane - 1].start()
             ride_both(step)
             step += 1
     for step in range(step, last + 1):
         ride_both(step)
+    for copy in writes:
+        copy.wait()
 
 
 def on_device(displacement, velocity, damage, broken, counts, bits):
     planes, rows, cells = damage.shape
     half = cells // 2
-    vmem = pl.BlockSpec(memory_space=pltpu.VMEM)
     smem = pl.BlockSpec(memory_space=pltpu.SMEM)
     hbm = pl.BlockSpec(memory_space=pltpu.HBM)
     f32, i32 = jnp.float32, jnp.int32
@@ -446,8 +465,9 @@
         kernel,
         out_shape=jax.ShapeDtypeStruct((6, planes, rows, cells), f32),
         in_specs=[smem] * 2 + [hbm] * 4,
-        out_specs=vmem,
+        out_specs=hbm,
         scratch_shapes=[
+            pltpu.VMEM((6, planes, rows, cells), f32),
             pltpu.VMEM((4, planes + 2, tall, cells), f32),
             pltpu.VMEM((2, planes, tall, cells), i32),
             pltpu.VMEM((3, planes, rows, cells), f32),
@@ -480,6 +500,7 @@
             pltpu.SemaphoreType.DMA((PIPES, 2, ROUNDS)),
             pltpu.SemaphoreType.DMA((PIPES, 2, ROUNDS)),
             pltpu.SemaphoreType.DMA((6,)),
+            pltpu.SemaphoreType.DMA((PIPES + planes - 1,)),
         ],
         compiler_params=pltpu.CompilerParams(
             collective_id=0, has_side_effects=True, vmem_limit_bytes=60 * 1024 * 1024

time: 61.1 us -> 60.6 us (level)
  no operation moved by 1% of the time
where the time goes in v6:
time: 60.6 us; the launch traced here: 60.4 us
  Pallas kernels  57.7 us (95%)
  local copies, waits for them, and re-layouts  2.7 us (4%)
    pallas_call x1, Pallas kernels, on_device(): pl.pallas_call(kernel, out_shape=jax.ShapeDtypeStruct((6, planes, rows, c...  57.7 us
    unnamed x1, local copies, waits for them, and re-layouts  2.7 us

profile of v6, /device:TPU:0, one launch (start us, length us, event | category | flops | bytes accessed | tf_op | source)
XLA Modules:
  0.0 60.4 jit_solution(16599433744719725917)
XLA Ops:
  0.0 57.7 %shard_map.64 = f32[6,4,64,256]{3,2,1,0:T(8,128)} custom-call(s32[4,16]{1,0:T(4,128)} %bitcast.1, s32[4]{0:T(128)} %bits.1, f32[3,4,64,256]{3,2,1,0:T(8,128)} %displacement.1, f32[3,4,64,256]{3,2,1,0:T(8,128)} %velocity_in.1, f32[4,64,256]{2,1,0:T(8,128)} %damage.1, s32[2,4,64,256]{3,2,1,0:T(8,128)} %broken.1), custom_call_target="tpu_custom_call" | custom-call | tf_op jit(solution)/shard_map/pallas_call | solution.py:464
  57.7 2.7 %copy.8 = f32[6,4,64,256]{3,2,1,0:T(8,128)} copy(f32[6,4,64,256]{3,2,1,0:T(8,128)} %shard_map.64) | data formatting | bytes 3145728
